TPU v7x, 32 devices: a whole 2x2x4 slice. The times are simulated.
32 devices in a mesh: seq: 8 (over z, y), chan: 4 (over x, core).
Axes of the slice: x: 2, y: 2, z: 4, core: 2. Of those that a mesh axis runs over, the one named last changes fastest.
Arguments:
- query_projected: bfloat16 [2048, 4096], P('seq', 'chan'), may hold values from -6 to 6
- key_stream: bfloat16 [2048, 4096], P('seq', 'chan'), may hold values from -6 to 6
- value_stream: bfloat16 [2048, 4096], P('seq', 'chan'), may hold values from -6 to 6
- short_taps: float32 [3, 3, 4096], P(None, None, 'chan'), may hold values from -3 to 3
- skip_gain: float32 [4096], P('chan'), may hold values from -4 to 4
- long_filter: float32 [2048, 4096], P('seq', 'chan'), may hold values from -4 to 4
- out_weight: bfloat16 [4096, 4096], P('chan'), may hold values from -0.09375 to 0.09375
Outputs:
- mixed: bfloat16 [2048, 4096], P('seq')
All inputs are finite; a program needn't handle non-finite values.
Results may differ from a plain program's by a relative error of at most 0.005.
Values may be sent and summed in bfloat16 or wider, within the bound.
A program may use at most 128 MiB of HBM per device.

v0:
```python
import math

import jax
import jax.numpy as jnp
from jax import lax
from jax.sharding import PartitionSpec as P

HIGH = lax.Precision.HIGHEST


def from_behind(array, axis, by):
    peers = lax.axis_size(axis)
    pairs = [(i, i + by) for i in range(peers) if 0 <= i + by < peers]
    return lax.ppermute(array, axis, pairs)


def from_partner(value, axis, stride):
    mask = 2**stride
    pairs = [(source, source ^ mask) for source in range(lax.axis_size(axis))]
    return lax.ppermute(value, axis, pairs)


def bit_reverse(place, seq_bits):
    result = jnp.zeros_like(place)
    for digit_count in range(seq_bits):
        result = result + ((place >> digit_count & 1) << seq_bits - 1 - digit_count)
    return result


def middle(real_part, imag_part, freq_low, seq_count, shard_len):
    padded_len = 2 * seq_count * shard_len
    steps_idx = jnp.arange(shard_len, dtype=jnp.int32)
    twist_turns = freq_low[:, None] * steps_idx[None, :] % padded_len
    twist_angle = twist_turns.astype(jnp.float32) * (2.0 * math.pi / padded_len)
    twist_cos = jnp.cos(twist_angle)[None, :, :, None]
    twist_sin = jnp.sin(twist_angle)[None, :, :, None]
    turned_real = real_part * twist_cos + imag_part * twist_sin
    turned_imag = imag_part * twist_cos - real_part * twist_sin
    shared_turns = steps_idx[:, None] * steps_idx[None, :] % shard_len
    shared_angle = shared_turns.astype(jnp.float32) * (2.0 * math.pi / shard_len)
    cosine = jnp.cos(shared_angle)
    sine = jnp.sin(shared_angle)
    spec_real = jnp.einsum("mn,fknc->fkmc", cosine, turned_real, precision=HIGH) + jnp.einsum(
        "mn,fknc->fkmc", sine, turned_imag, precision=HIGH
    )
    spec_imag = jnp.einsum("mn,fknc->fkmc", cosine, turned_imag, precision=HIGH) - jnp.einsum(
        "mn,fknc->fkmc", sine, turned_real, precision=HIGH
    )
    prod_real = spec_real[0] * spec_real[1] - spec_imag[0] * spec_imag[1]
    prod_imag = spec_real[0] * spec_imag[1] + spec_imag[0] * spec_real[1]
    summed_real = jnp.einsum("mn,kmc->knc", cosine, prod_real, precision=HIGH) - jnp.einsum(
        "mn,kmc->knc", sine, prod_imag, precision=HIGH
    )
    imaginary_summed = jnp.einsum("mn,kmc->knc", cosine, prod_imag, precision=HIGH) + jnp.einsum(
        "mn,kmc->knc", sine, prod_real, precision=HIGH
    )
    back_real = summed_real * twist_cos[0] - imaginary_summed * twist_sin[0]
    back_imag = imaginary_summed * twist_cos[0] + summed_real * twist_sin[0]
    return (back_real, back_imag)


def on_device(
    query_projected, key_stream, value_stream, short_taps, skip_gain, long_filter, out_weight
):
    shard_len = query_projected.shape[0]
    seq_count = lax.axis_size("seq")
    seq_bits = seq_count.bit_length() - 1
    padded_len = 2 * seq_count * shard_len
    place = lax.axis_index("seq")
    pair_idx = jnp.arange(2, dtype=jnp.int32)
    streams = jnp.stack([query_projected, key_stream, value_stream])
    rim_rows = from_behind(streams[:, -2:, :], "seq", 1)
    extended = jnp.concatenate([rim_rows, streams], axis=1).astype(jnp.float32)
    shaped = (
        short_taps[0][:, None, :] * extended[:, 2:]
        + short_taps[1][:, None, :] * extended[:, 1:-1]
        + short_taps[2][:, None, :] * extended[:, :-2]
    )
    source = shaped[1] * shaped[2]
    fields = jnp.stack([source, long_filter])
    base_angle = place.astype(jnp.float32) * (math.pi / seq_count)
    base_cos = jnp.cos(base_angle)
    base_sin = jnp.sin(base_angle)
    real_part = jnp.stack([fields, fields * base_cos], axis=1)
    imag_part = jnp.stack([jnp.zeros_like(fields), -fields * base_sin], axis=1)
    values = jnp.stack([real_part, imag_part])
    for section_bit in reversed(range(seq_bits)):
        half_span = 1 << section_bit
        partner = from_partner(values, "seq", section_bit)
        upper_side = place >> section_bit & 1 == 1
        angle = (place % half_span).astype(jnp.float32) * (math.pi / half_span)
        cosine = jnp.cos(angle)
        sine = jnp.sin(angle)
        gap_value = partner - values
        upper = jnp.stack(
            [
                gap_value[0] * cosine + gap_value[1] * sine,
                gap_value[1] * cosine - gap_value[0] * sine,
            ]
        )
        values = jnp.where(upper_side, upper, values + partner)
    freq_low = 2 * bit_reverse(place, seq_bits) + pair_idx
    back_real, back_imag = middle(values[0], values[1], freq_low, seq_count, shard_len)
    values = jnp.stack([back_real, back_imag])
    for section_bit in range(seq_bits):
        half_span = 1 << section_bit
        partner = from_partner(values, "seq", section_bit)
        upper_side = place >> section_bit & 1 == 1
        angle = (place % half_span).astype(jnp.float32) * (math.pi / half_span)
        cosine = jnp.cos(angle)
        sine = jnp.sin(angle)

        def rotate(field):
            return jnp.stack(
                [cosine * field[0] - sine * field[1], cosine * field[1] + sine * field[0]]
            )

        values = jnp.where(upper_side, partner - rotate(values), values + rotate(partner))
    convolved = (values[0, 0] + base_cos * values[0, 1] - base_sin * values[1, 1]) / padded_len
    gated = (shaped[0] * (convolved + skip_gain[None, :] * source)).astype(jnp.bfloat16)
    terms = jnp.dot(gated, out_weight, preferred_element_type=jnp.float32)
    mixed = lax.psum(terms, "chan").astype(jnp.bfloat16)
    return mixed


def solution(mesh):
    return jax.shard_map(
        on_device,
        mesh=mesh,
        in_specs=(
            P("seq", "chan"),
            P("seq", "chan"),
            P("seq", "chan"),
            P(None, None, "chan"),
            P("chan"),
            P("seq", "chan"),
            P("chan", None),
        ),
        out_specs=P("seq", None),
        check_vma=False,
    )
```

profile of v0, /device:TPU:29, one launch (start us, length us, event | category | flops | bytes accessed | tf_op | source)
XLA Modules:
  0.0 1326.0 jit_solution(10734665954037668456)
XLA Ops:
  10.2 3.7 fusion.3
  16.5 4.2 pad_maximum_fusion
  23.1 362.2 %collective-permute-done.1 = f32[2,2,2,256,1024]{3,4,2,1,0:T(8,128)} collective-permute-done((f32[2,2,2,256,1024]{3,4,2,1,0:T(8,128)}, f32[2,2,2,256,1024]{3,4,2,1,0:T(8,128)}, u32[]{:S(2)}, u32[]{:S(2)}) %collective-permute-start.1) | collective-permute-done | bytes 8388640 | tf_op jit(solution)/shard_map/ppermute | solution.py:20
  385.3 9.9 fusion.100
  395.2 4.5 multiply_add_fusion.3
  402.0 7.1 maximum_select_fusion
  409.4 181.2 %collective-permute-done.2 = f32[2,2,2,256,1024]{3,4,2,1,0:T(8,128)} collective-permute-done((f32[2,2,2,256,1024]{3,4,2,1,0:T(8,128)}, f32[2,2,2,256,1024]{3,4,2,1,0:T(8,128)}, u32[]{:S(2)}, u32[]{:S(2)}) %collective-permute-start.2) | collective-permute-done | bytes 8388640 | tf_op jit(solution)/shard_map/ppermute | solution.py:20
  590.5 15.3 %fusion.106 = f32[2,2,2,256,1024]{3,4,2,1,0:T(8,128)} fusion(f32[2,2,2,256,1024]{3,4,2,1,0:T(8,128)} %collective-permute-done.2, f32[2,2,2,256,1024]{3,4,2,1,0:T(8,128)} %collective-permute-done.1, f32[1,2,2,256,1024]{3,4,2,1,0:T(8,128)} %copy-done.3, f32[1,2,2,256,1024]{3,4,2,1,0:T(8,128)} %copy-done, f32[1,2,2,256,1024]{3,4,2,1,0:T(8,128)} %copy-done.7, ...), kind=kLoop, calls=%fused_computation.154 | loop fusion | flops 10485760 | bytes 41943040 | tf_op jit(solution)/shard_map/sub | solution.py:94
  605.8 7.9 multiply_add_fusion.2
  613.7 17.0 %maximum_select_fusion.1 = f32[2,2,2,256,1024]{3,4,2,1,0:T(8,128)} fusion(f32[1,2,2,256,1024]{3,4,2,1,0:T(8,128)} %get-tuple-element.13, f32[1,2,2,256,1024]{3,4,2,1,0:T(8,128)} %get-tuple-element.12, f32[2,2,2,256,1024]{3,4,2,1,0:T(8,128)} %collective-permute-done.2, pred[]{:T(512)S(6)} %eq.24, f32[2,2,2,256,1024]{3,4,2,1,0:T(8,128)} %collective-permute-done.1, ...), kind=kLoop, calls=%fused_computation.2 | loop fusion | flops 14680064 | bytes 50331648 | tf_op jit(solution)/shard_map/jit(_where)/select_n | solution.py:101
  632.7 179.3 %collective-permute-done.3 = f32[2,2,2,256,1024]{3,4,2,1,0:T(8,128)} collective-permute-done((f32[2,2,2,256,1024]{3,4,2,1,0:T(8,128)}, f32[2,2,2,256,1024]{3,4,2,1,0:T(8,128)}, u32[]{:S(2)}, u32[]{:S(2)}) %collective-permute-start.3) | collective-permute-done | bytes 8388640 | tf_op jit(solution)/shard_map/ppermute | solution.py:20
  812.1 10.1 sub.86
  822.1 6.3 multiply_add_fusion.1
  829.5 5.6 maximum_select_fusion.2
  835.1 4.7 fusion.31
  839.9 4.7 fusion.30
  844.6 5.1 add_bitcast_fusion
  849.6 4.8 subtract_bitcast_fusion
  869.5 88.1 %collective-permute-done.4 = f32[2,2,256,1024]{2,3,1,0:T(8,128)S(1)} collective-permute-done((f32[2,2,256,1024]{2,3,1,0:T(8,128)S(1)}, f32[2,2,256,1024]{2,3,1,0:T(8,128)S(1)}, u32[]{:S(2)}, u32[]{:S(2)}) %collective-permute-start.4) | collective-permute-done | bytes 4194336 | tf_op jit(solution)/shard_map/ppermute | solution.py:20
  962.5 85.4 %collective-permute-done.5 = f32[2,2,256,1024]{2,3,1,0:T(8,128)S(1)} collective-permute-done((f32[2,2,256,1024]{2,3,1,0:T(8,128)S(1)}, f32[2,2,256,1024]{2,3,1,0:T(8,128)S(1)}, u32[]{:S(2)}, u32[]{:S(2)}) %collective-permute-start.5) | collective-permute-done | bytes 4194336 | tf_op jit(solution)/shard_map/ppermute | solution.py:20
  1051.4 5.6 fusion.1
  1057.5 181.7 %collective-permute-done.6 = f32[2,2,256,1024]{2,3,1,0:T(8,128)S(1)} collective-permute-done((f32[2,2,256,1024]{2,3,1,0:T(8,128)S(1)}, f32[2,2,256,1024]{2,3,1,0:T(8,128)S(1)}, u32[]{:S(2)}, u32[]{:S(2)}) %collective-permute-start.6) | collective-permute-done | bytes 4194336 | tf_op jit(solution)/shard_map/ppermute | solution.py:20
  1243.7 4.8 fusion.32
  1248.4 77.3 %all-reduce.2 = bf16[256,4096]{1,0:T(8,128)(2,1)} all-reduce(f32[256,4096]{1,0:T(8,128)} %fusion.32), channel_id=1, replica_groups=mesh['seq'=8,'chan'=4] {'chan'}, use_global_device_ids=true, to_apply=%region_0.1 | all-reduce | flops 1048576 | bytes 6291456 | tf_op jit(solution)/shard_map/psum | solution.py:122
  (69 shorter events, 48.6 us)
Async XLA Ops:
  0.0 5.6 copy-start.12
  4.3 4.4 collective-permute-start
  13.9 1.7 copy-start.8
  16.5 4.5 copy-start
  16.5 5.8 copy-start.3
  22.4 362.9 %collective-permute-start.1 = (f32[2,2,2,256,1024]{3,4,2,1,0:T(8,128)}, f32[2,2,2,256,1024]{3,4,2,1,0:T(8,128)}, u32[]{:S(2)}, u32[]{:S(2)}) collective-permute-start(f32[2,2,2,256,1024]{3,4,2,1,0:T(8,128)} %pad_maximum_fusion), channel_id=1, source_target_pairs={{0,16},{4,20},{8,24},{12,28},{16,0},{20,4},{24,8},{28,12},{1,17},{... | collective-permute-start | bytes 25165832 | tf_op jit(solution)/shard_map/ppermute | solution.py:20
  395.2 4.6 copy-start.1
  395.2 6.8 copy-start.4
  399.7 9.5 copy-start.6
  399.7 9.5 copy-start.7
  409.2 181.4 %collective-permute-start.2 = (f32[2,2,2,256,1024]{3,4,2,1,0:T(8,128)}, f32[2,2,2,256,1024]{3,4,2,1,0:T(8,128)}, u32[]{:S(2)}, u32[]{:S(2)}) collective-permute-start(f32[2,2,2,256,1024]{3,4,2,1,0:T(8,128)} %maximum_select_fusion), channel_id=1, source_target_pairs={{0,8},{4,12},{8,0},{12,4},{16,24},{20,28},{24,16},{28,20},{1,9},{5... | collective-permute-start | bytes 25165832 | tf_op jit(solution)/shard_map/ppermute | solution.py:20
  605.8 7.9 copy-start.2
  630.7 181.4 %collective-permute-start.3 = (f32[2,2,2,256,1024]{3,4,2,1,0:T(8,128)}, f32[2,2,2,256,1024]{3,4,2,1,0:T(8,128)}, u32[]{:S(2)}, u32[]{:S(2)}) collective-permute-start(f32[2,2,2,256,1024]{3,4,2,1,0:T(8,128)} %maximum_select_fusion.1), channel_id=1, source_target_pairs={{0,4},{4,0},{8,12},{12,8},{16,20},{20,16},{24,28},{28,24},{1,5},{5... | collective-permute-start | bytes 25165832 | tf_op jit(solution)/shard_map/ppermute | solution.py:20
  822.1 7.3 copy-start.5
  867.6 89.9 %collective-permute-start.4 = (f32[2,2,256,1024]{2,3,1,0:T(8,128)S(1)}, f32[2,2,256,1024]{2,3,1,0:T(8,128)S(1)}, u32[]{:S(2)}, u32[]{:S(2)}) collective-permute-start(f32[2,2,256,1024]{2,3,1,0:T(8,128)S(1)} %pad_maximum_fusion.1), channel_id=1, source_target_pairs={{0,4},{4,0},{8,12},{12,8},{16,20},{20,16},{24,28},{28,24},{1,5},{5... | collective-permute-start | bytes 12582920 | tf_op jit(solution)/shard_map/ppermute | solution.py:20
  959.0 89.0 %collective-permute-start.5 = (f32[2,2,256,1024]{2,3,1,0:T(8,128)S(1)}, f32[2,2,256,1024]{2,3,1,0:T(8,128)S(1)}, u32[]{:S(2)}, u32[]{:S(2)}) collective-permute-start(f32[2,2,256,1024]{2,3,1,0:T(8,128)S(1)} %fusion), channel_id=1, source_target_pairs={{0,8},{4,12},{8,0},{12,4},{16,24},{20,28},{24,16},{28,20},{1,9},{5... | collective-permute-start | bytes 12582920 | tf_op jit(solution)/shard_map/ppermute | solution.py:20
  1048.0 3.4 copy-start.10
  1056.9 182.3 %collective-permute-start.6 = (f32[2,2,256,1024]{2,3,1,0:T(8,128)S(1)}, f32[2,2,256,1024]{2,3,1,0:T(8,128)S(1)}, u32[]{:S(2)}, u32[]{:S(2)}) collective-permute-start(f32[2,2,256,1024]{2,3,1,0:T(8,128)S(1)} %fusion.1), channel_id=1, source_target_pairs={{0,16},{4,20},{8,24},{12,28},{16,0},{20,4},{24,8},{28,12},{1,17},{... | collective-permute-start | bytes 12582920 | tf_op jit(solution)/shard_map/ppermute | solution.py:20
  1239.2 2.2 slice-start
  1239.6 2.8 copy-start.9
  1239.7 4.0 slice-start.1
  1239.7 4.0 copy-start.11
where the time goes:
time: 1330 us
  waiting for transfers between devices  1080 us (81%)
  other arithmetic  110 us (8%)
  blocking collectives  77.3 us (6%)
  matrix products  36.3 us (3%)
  local copies, waits for them, and re-layouts  15.5 us (1%)
    ppermute x6, waiting for transfers between devices, from_partner(): return lax.ppermute(value, axis, pairs)  1080 us
    psum x1, blocking collectives, on_device(): mixed = lax.psum(terms, 'chan').astype(jnp.bfloat16)  77.3 us
    sub x3, other arithmetic, on_device(): gap_value = partner - values  35.2 us
    select_n x3, other arithmetic, on_device(): values = jnp.where(upper_side, upper, values + partner)  29.7 us
  transfers between devices with their start and end apart: 7, of which 7 were waited for; matrix products, arithmetic and copies ran while one was open for 0% of the time, Pallas kernels for 0%

commit v1 on v0

v1 whole, which is shorter than its diff:
```python
import jax
import jax.numpy as jnp
import numpy as np
import ml_dtypes
from jax import lax
from jax.sharding import PartitionSpec as P


def transform(seq_len):
    period = 4 * seq_len
    freq = 2 * np.arange(seq_len, dtype=np.int64) + 1
    turns = freq[:, None] * np.arange(seq_len, dtype=np.int64)[None, :] % period
    angle = np.arange(period) * (2.0 * np.pi / period)
    table = np.stack([np.cos(angle), np.sin(angle)]).astype(ml_dtypes.bfloat16)
    return table[:, turns].reshape(2 * seq_len, seq_len)


def from_behind(array, axis, by):
    peers = lax.axis_size(axis)
    pairs = [(i, i + by) for i in range(peers) if 0 <= i + by < peers]
    return lax.ppermute(array, axis, pairs)


def on_device(
    matrix,
    query_projected,
    key_stream,
    value_stream,
    short_taps,
    skip_gain,
    long_filter,
    out_weight,
):
    shard_len, width = query_projected.shape
    seq_count = lax.axis_size("seq")
    seq_len = seq_count * shard_len
    part = width // seq_count
    streams = [query_projected, key_stream, value_stream]
    rims = from_behind(jnp.stack([x[-2:] for x in streams]), "seq", 1)

    def shape_stream(index):
        ext = jnp.concatenate([rims[index], streams[index]], axis=0).astype(jnp.float32)
        return (
            short_taps[0, index] * ext[2:]
            + short_taps[1, index] * ext[1:-1]
            + short_taps[2, index] * ext[:-2]
        )

    source = shape_stream(1) * shape_stream(2)
    fields = jnp.stack([source.astype(jnp.bfloat16), long_filter.astype(jnp.bfloat16)])
    fields = fields.reshape(2, shard_len, seq_count, part).transpose(2, 1, 0, 3)
    fields = fields.reshape(seq_count, shard_len, 2 * part)
    fields = lax.all_to_all(fields, "seq", 0, 0, tiled=True).reshape(seq_len, 2 * part)
    spec = jnp.dot(matrix, fields, preferred_element_type=jnp.float32)
    real, imag = spec[:seq_len], spec[seq_len:]
    a, b = real[:, :part], real[:, part:]
    c, d = imag[:, :part], imag[:, part:]
    prod = jnp.concatenate([a * b - c * d, a * d + c * b]) * (1.0 / seq_len)
    convolved = lax.dot_general(
        matrix,
        prod.astype(jnp.bfloat16),
        (((0,), (0,)), ((), ())),
        preferred_element_type=jnp.float32,
    ).astype(jnp.bfloat16)
    convolved = convolved.reshape(seq_count, shard_len, part)
    convolved = lax.all_to_all(convolved, "seq", 0, 0, tiled=True)
    convolved = convolved.transpose(1, 0, 2).reshape(shard_len, width).astype(jnp.float32)
    gated = (shape_stream(0) * (convolved + skip_gain * source)).astype(jnp.bfloat16)
    terms = jnp.dot(gated, out_weight, preferred_element_type=jnp.float32)
    return lax.psum(terms.astype(jnp.bfloat16), "chan")


def solution(mesh):
    mapped = jax.shard_map(
        on_device,
        mesh=mesh,
        in_specs=(
            P(None, None),
            P("seq", "chan"),
            P("seq", "chan"),
            P("seq", "chan"),
            P(None, None, "chan"),
            P("chan"),
            P("seq", "chan"),
            P("chan", None),
        ),
        out_specs=P("seq", None),
        check_vma=False,
    )

    def run(*arrays):
        return mapped(transform(arrays[0].shape[0]), *arrays)

    return run
```

time: 1330 us -> 151 us (0.11)
  waiting for transfers between devices: 1080 us -> 65.6 us
  other arithmetic: 110 us -> 3.89 us
  blocking collectives: 77.3 us -> 28.9 us
  matrix products: 36.3 us -> 21.1 us
    ppermute x6 -> x0, waiting for transfers between devices: 1080 us -> none  [from_partner(): return lax.ppermute(value, axis, pairs)]
    psum x1 -> x0, blocking collectives: 77.3 us -> none  [on_device(): mixed = lax.psum(terms, 'chan').astype(jnp.bfloat16)]
    psum x0 -> x1, waiting for transfers between devices: none -> 52.6 us  [on_device(): return lax.psum(terms.astype(jnp.bfloat16), 'chan')]
    sub x9 -> x1, other arithmetic: 42.3 us -> 0.22 us  [on_device(): prod = jnp.concatenate([a * b - c * d, a * d + c * b]) * (1.0 / seq_len)]
    select_n x6 -> x0, other arithmetic: 37.8 us -> none  [the longest x3 29.7 us: on_device(): values = jnp.where(upper_side, upper, values + partner)]
    all_to_all x0 -> x1, blocking collectives: none -> 28.9 us  [on_device(): lax.all_to_all(fields, 'seq', 0, 0, tiled=True).reshape(seq_len, 2 * part)]
    add x5 -> x0, other arithmetic: 22.4 us -> none  [the longest x3 18.8 us: on_device(): gap_value[0] * cosine + gap_value[1] * sine]
    dot_general x8 -> x2, matrix products: 31.5 us -> 13.1 us  [the longest x1 10.8 us: on_device(): spec = jnp.dot(matrix, fields, preferred_element_type=jnp.float32)]
  transfers between devices with their start and end apart: 7 -> 3, of which waited for: 7 -> 3; matrix products, arithmetic and copies ran while one was open for 0% -> 2% of each run, Pallas kernels for 0% -> 0%
where the time goes in v1:
time: 151 us; the launch traced here: 149 us
  waiting for transfers between devices  65.6 us (43%)
  blocking collectives  28.9 us (19%)
  matrix products  21.1 us (14%)
  between operations  13.6 us (9%)
  local copies, waits for them, and re-layouts  8.71 us (6%)
  starting transfers between devices  6.73 us (4%)
  other arithmetic  3.89 us (3%)
    psum x1, waiting for transfers between devices, on_device(): return lax.psum(terms.astype(jnp.bfloat16), 'chan')  52.6 us
    all_to_all x1, blocking collectives, on_device(): lax.all_to_all(fields, 'seq', 0, 0, tiled=True).reshape(seq_len, 2 * part)  28.9 us
    all_to_all x1, waiting for transfers between devices, on_device(): convolved = lax.all_to_all(convolved, 'seq', 0, 0, tiled=True)  12.3 us
    dot_general x1, matrix products, on_device(): spec = jnp.dot(matrix, fields, preferred_element_type=jnp.float32)  10.8 us
    dot_general x1, matrix products, on_device(): terms = jnp.dot(gated, out_weight, preferred_element_type=jnp.float32)  7.92 us
    all_to_all x1, starting transfers between devices, on_device(): convolved = lax.all_to_all(convolved, 'seq', 0, 0, tiled=True)  5.44 us
    unnamed x17, local copies, waits for them, and re-layouts  3.18 us
  transfers between devices with their start and end apart: 3, of which 3 were waited for; matrix products, arithmetic and copies ran while one was open for 2% of the time, Pallas kernels for 0%

profile of v1, /device:TPU:29, one launch (start us, length us, event | category | flops | bytes accessed | tf_op | source)
XLA Modules:
  0.0 148.5 jit_solution(17423483335536082827)
XLA Ops:
  6.5 0.8 slice_bitcast_fusion.5
  7.3 0.7 slice_bitcast_fusion.3
  8.1 1.3 collective-permute-start
  9.4 0.9 fusion.21
  10.3 1.4 convert_element_type.43
  11.7 0.2 copy.18
  11.9 0.6 collective-permute-done
  12.6 0.1 maximum_convert_fusion.1
  12.7 0.1 maximum_convert_fusion.2
  12.9 1.7 %fusion.19 = (bf16[256,1024]{1,0:T(8,128)(2,1)S(1)}, f32[256,1024]{1,0:T(8,128)}) fusion(f32[258,1024]{1,0:T(8,128)S(1)} %maximum_convert_fusion.2, f32[1024]{0:T(1024)S(1)} %bitcast.51, f32[1024]{0:T(1024)S(1)} %bitcast.52, f32[1024]{0:T(1024)S(1)} %bitcast.47, f32[258,1024]{1,0:T(8,128)S(1)} %maximum_convert_fusion.1, f32[1024]{0:T(1024)S(1)} %bitcast.48, ...), kind=kLoop, calls=%fused_computation.43 | loop fusion | flops 3145728 | bytes 7888896 | tf_op jit(solution)/shard_map/convert_element_type | solution.py:50
  14.5 0.2 copy.17
  14.9 28.9 %all_to_all.10 = bf16[8,256,256]{1,2,0:T(8,128)(2,1)S(1)} all-to-all(bf16[8,256,256]{1,2,0:T(8,128)(2,1)S(1)} %bitcast.41), channel_id=1, replica_groups=mesh['seq'=8,'chan'=4] {'seq'}, dimensions={0} | all-to-all | bytes 2097152 | tf_op jit(solution)/shard_map/all_to_all | solution.py:53
  43.8 0.5 copy.19
  44.4 10.8 %fusion.22 = f32[4096,256]{1,0:T(8,128)S(1)} fusion(bf16[4096,2048]{1,0:T(8,128)(2,1)} %constant.4.clone, bf16[2048,256]{1,0:T(8,128)(2,1)S(1)} %bitcast.46), kind=kOutput, calls=%fused_computation.45 | convolution fusion | flops 4294967296 | bytes 22020096 | tf_op jit(solution)/shard_map/dot_general | solution.py:54
  55.2 0.2 multiply_subtract_fusion
  55.4 2.4 %convolution_convert_fusion.1 = bf16[128,2048]{1,0:T(8,128)(2,1)S(1)} fusion(bf16[4096,2048]{1,0:T(8,128)(2,1)S(1)} %bitcast.40, f32[2048,128]{1,0:T(8,128)S(1)} %get-tuple-element.8, f32[2048,128]{1,0:T(8,128)S(1)} %get-tuple-element.7), kind=kOutput, calls=%fused_computation.1 | convolution fusion | flops 2149318656 | bytes 19398656 | tf_op jit(solution)/shard_map/dot_general | solution.py:59
  57.8 0.8 copy.24
  58.7 5.4 %all-to-all-start.1 = ((bf16[8,256,128]{1,2,0:T(8,128)(2,1)}), bf16[8,256,128]{1,2,0:T(8,128)(2,1)S(1)}, u32[]{:S(2)}, u32[]{:S(2)}) async-start(bf16[8,256,128]{1,2,0:T(8,128)(2,1)} %bitcast.38), calls=%async_computation.1 | async-start | bytes 1048576 | tf_op jit(solution)/shard_map/all_to_all | solution.py:66
  64.1 0.1 maximum_convert_fusion
  64.3 12.3 %all-to-all-done.1 = bf16[8,256,128]{1,2,0:T(8,128)(2,1)S(1)} async-done(((bf16[8,256,128]{1,2,0:T(8,128)(2,1)}), bf16[8,256,128]{1,2,0:T(8,128)(2,1)S(1)}, u32[]{:S(2)}, u32[]{:S(2)}) %all-to-all-start.1) | async-done | bytes 524320 | tf_op jit(solution)/shard_map/all_to_all | solution.py:66
  76.7 1.3 copy.21
  78.0 7.9 %convolution_convert_fusion = bf16[256,4096]{1,0:T(8,128)(2,1)} fusion(bf16[1024,4096]{1,0:T(8,128)(2,1)} %param.14, f32[258,1024]{1,0:T(8,128)S(1)} %maximum_convert_fusion, f32[256,1024]{1,0:T(8,128)} %copy.21, f32[256,1024]{1,0:T(8,128)} %get-tuple-element.6, f32[1024]{0:T(1024)S(1)} %copy-done.3, f32[1024]{0:T(1024)S(1)} %bitcast.54, ...), kind=kOutput, calls=%fused_computation | convolution fusion | flops 2150891520 | bytes 15745024 | tf_op jit(solution)/shard_map/dot_general | solution.py:69
  85.9 52.6 %all-reduce.2.cloned.1.call-done = bf16[256,4096]{1,0:T(8,128)(2,1)} async-done(((bf16[256,4096]{1,0:T(8,128)(2,1)}), bf16[256,4096]{1,0:T(8,128)(2,1)}) %all-reduce.2.cloned.1.call-update) | async-done | bytes 2097168 | tf_op jit(solution)/shard_map/psum | solution.py:70
  138.6 3.1 %copy.26 = bf16[256,4096]{1,0:T(8,128)(2,1)} copy(bf16[256,4096]{1,0:T(8,128)(2,1)} %all-reduce.2.cloned.1.call-done) | data formatting | bytes 4194304
  (23 shorter events, 0.3 us)
Async XLA Ops:
  6.5 6.0 %copy-start = (bf16[256,1024]{1,0:T(8,128)(2,1)S(1)}, bf16[256,1024]{1,0:T(8,128)(2,1)}, u32[]{:S(2)}) copy-start(bf16[256,1024]{1,0:T(8,128)(2,1)} %param.9) | copy-start | bytes 1572868
  8.1 4.4 %collective-permute-start = (bf16[3,2,1024]{2,1,0:T(2,128)(2,1)S(1)}, bf16[3,2,1024]{2,1,0:T(2,128)(2,1)S(1)}, u32[]{:S(2)}, u32[]{:S(2)}) collective-permute-start(bf16[3,2,1024]{2,1,0:T(2,128)(2,1)S(1)} %pad_maximum_fusion.1), channel_id=1, source_target_pairs={{0,4},{4,8},{8,12},{12,16},{16,20},{20,24},{24,28},{1,5},{5,9},{9,... | collective-permute-start | bytes 36872 | tf_op jit(solution)/shard_map/ppermute | solution.py:21
  10.3 2.4 %copy-start.1 = (bf16[256,1024]{1,0:T(8,128)(2,1)S(1)}, bf16[256,1024]{1,0:T(8,128)(2,1)}, u32[]{:S(2)}) copy-start(bf16[256,1024]{1,0:T(8,128)(2,1)} %param.10) | copy-start | bytes 1572868
  44.3 11.1 %slice-start = ((s8[16777216]{0:T(1024)(128)(4,1)}), s8[4194304]{0:T(1024)(128)(4,1)S(1)}, s32[]{:S(2)}) async-start(s8[16777216]{0:T(1024)(128)(4,1)} %bitcast.39), calls=%async_computation.3 | async-start | bytes 8388608
  44.3 11.1 %slice-start.1 = ((s8[16777216]{0:T(1024)(128)(4,1)}), s8[4194304]{0:T(1024)(128)(4,1)S(1)}, s32[]{:S(2)}) async-start(s8[16777216]{0:T(1024)(128)(4,1)} %bitcast.39), calls=%async_computation.4 | async-start | bytes 8388608
  44.4 11.1 %slice-start.2 = ((s8[16777216]{0:T(1024)(128)(4,1)}), s8[4194304]{0:T(1024)(128)(4,1)S(1)}, s32[]{:S(2)}) async-start(s8[16777216]{0:T(1024)(128)(4,1)} %bitcast.39), calls=%async_computation.5 | async-start | bytes 8388608
  44.4 11.1 %slice-start.3 = ((s8[16777216]{0:T(1024)(128)(4,1)}), s8[4194304]{0:T(1024)(128)(4,1)S(1)}, s32[]{:S(2)}) async-start(s8[16777216]{0:T(1024)(128)(4,1)} %bitcast.39), calls=%async_computation.6 | async-start | bytes 8388608
  57.8 6.3 %copy-start.2 = (bf16[256,1024]{1,0:T(8,128)(2,1)S(1)}, bf16[256,1024]{1,0:T(8,128)(2,1)}, u32[]{:S(2)}) copy-start(bf16[256,1024]{1,0:T(8,128)(2,1)} %param.8) | copy-start | bytes 1572868
  58.7 17.9 %all-to-all-start.1 = ((bf16[8,256,128]{1,2,0:T(8,128)(2,1)}), bf16[8,256,128]{1,2,0:T(8,128)(2,1)S(1)}, u32[]{:S(2)}, u32[]{:S(2)}) async-start(bf16[8,256,128]{1,2,0:T(8,128)(2,1)} %bitcast.38), calls=%async_computation.1 | async-start | bytes 1048576 | tf_op jit(solution)/shard_map/all_to_all | solution.py:66
  64.1 74.5 %all-reduce.2.cloned.1.call-start = ((), (), s32[]{:S(2)}) async-start(), calls=%async_computation.2 | async-start | bytes 4194304 | tf_op jit(solution)/shard_map/psum | solution.py:70
  64.3 13.7 %copy-start.3 = (f32[1024]{0:T(1024)S(1)}, f32[1024]{0:T(1024)}, u32[]{:S(2)}) copy-start(f32[1024]{0:T(1024)} %param.12) | copy-start | bytes 12292
Sparse Core Ops, SparseCore 0:
  86.1 52.4 all-reduce.1

commit v2 on v1

--- a/solution.py
+++ b/solution.py
@@ -1,8 +1,12 @@
+import functools
+
 import jax
 import jax.numpy as jnp
 import numpy as np
 import ml_dtypes
 from jax import lax
+from jax.experimental import pallas as pl
+from jax.experimental.pallas import tpu as pltpu
 from jax.sharding import PartitionSpec as P
 
 
@@ -19,6 +23,162 @@
     peers = lax.axis_size(axis)
     pairs = [(i, i + by) for i in range(peers) if 0 <= i + by < peers]
     return lax.ppermute(array, axis, pairs)
+
+
+CHUNKS = 4
+MESH = pl.DeviceIdType.MESH
+
+
+def project_kernel(
+    rounds,
+    gated_ref,
+    weight_ref,
+    out_ref,
+    weight,
+    core_send,
+    core_recv,
+    chip_send,
+    chip_recv,
+    weight_sem,
+    core_send_sem,
+    core_recv_sem,
+    chip_send_sem,
+    chip_recv_sem,
+    out_send_sem,
+    out_recv_sem,
+):
+    me = lax.axis_index("chan")
+    core = lax.rem(me, 2)
+    mate = me + 1 - 2 * core
+    half = out_ref.shape[1] // 2
+    wide = half // CHUNKS
+
+    def chip_peer(step):
+        stride = 2 << step
+        return me + stride * (1 - 2 * lax.rem(me // stride, 2))
+
+    def cols(side, j):
+        return pl.ds(pl.multiple_of(side * half + j * wide, wide), wide)
+
+    def weight_copy(turn, j):
+        side = core if turn else 1 - core
+        return pltpu.make_async_copy(
+            weight_ref.at[:, cols(side, j)], weight.at[:, cols(side, j)], weight_sem.at[turn, j]
+        )
+
+    def core_copy(j):
+        return pltpu.make_async_remote_copy(
+            src_ref=core_send.at[j],
+            dst_ref=core_recv.at[j],
+            send_sem=core_send_sem.at[j],
+            recv_sem=core_recv_sem.at[j],
+            device_id={"chan": mate},
+            device_id_type=MESH,
+        )
+
+    def chip_copy(step, j):
+        return pltpu.make_async_remote_copy(
+            src_ref=chip_send.at[step, j],
+            dst_ref=chip_recv.at[step, j],
+            send_sem=chip_send_sem.at[step, j],
+            recv_sem=chip_recv_sem.at[step, j],
+            device_id={"chan": chip_peer(step)},
+            device_id_type=MESH,
+        )
+
+    def out_copy(side, j):
+        return pltpu.make_async_remote_copy(
+            src_ref=out_ref.at[:, cols(side, j)],
+            dst_ref=out_ref.at[:, cols(side, j)],
+            send_sem=out_send_sem.at[j],
+            recv_sem=out_recv_sem.at[j],
+            device_id={"chan": mate},
+            device_id_type=MESH,
+        )
+
+    for turn in range(2):
+        for j in range(CHUNKS):
+            weight_copy(turn, j).start()
+    barrier = pltpu.get_barrier_semaphore()
+    for peer in [mate] + [chip_peer(step) for step in range(rounds)]:
+        pl.semaphore_signal(barrier, inc=1, device_id={"chan": peer}, device_id_type=MESH)
+    pl.semaphore_wait(barrier, 1 + rounds)
+
+    def part(turn, j):
+        weight_copy(turn, j).wait()
+        side = core if turn else 1 - core
+        return jnp.dot(
+            gated_ref[...], weight[:, cols(side, j)], preferred_element_type=jnp.float32
+        )
+
+    @pl.loop(0, CHUNKS)
+    def _(j):
+        core_send[j] = part(0, j)
+        core_copy(j).start()
+
+    @pl.loop(0, CHUNKS)
+    def _(j):
+        own = part(1, j)
+        core_copy(j).wait_recv()
+        chip_send[0, j] = (own + core_recv[j]).astype(jnp.bfloat16)
+        chip_copy(0, j).start()
+
+    for step in range(rounds):
+
+        @pl.loop(0, CHUNKS)
+        def _(j):
+            chip_copy(step, j).wait_recv()
+            total = chip_send[step, j].astype(jnp.float32) + chip_recv[step, j].astype(jnp.float32)
+            total = total.astype(jnp.bfloat16)
+            if step + 1 < rounds:
+                chip_send[step + 1, j] = total
+                chip_copy(step + 1, j).start()
+            else:
+                out_ref[:, cols(core, j)] = total
+                out_copy(core, j).start()
+
+    @pl.loop(0, CHUNKS)
+    def _(j):
+        core_copy(j).wait_send()
+        for step in range(rounds):
+            chip_copy(step, j).wait_send()
+        out_copy(core, j).wait_send()
+        out_copy(1 - core, j).wait_recv()
+
+
+def project(gated, out_weight):
+    rows, depth = gated.shape
+    columns = out_weight.shape[1]
+    wide = columns // 2 // CHUNKS
+    rounds = (lax.axis_size("chan") // 2).bit_length() - 1
+    return pl.pallas_call(
+        functools.partial(project_kernel, rounds),
+        out_shape=jax.ShapeDtypeStruct((rows, columns), jnp.bfloat16),
+        in_specs=[pl.BlockSpec(memory_space=pltpu.VMEM), pl.BlockSpec(memory_space=pl.ANY)],
+        out_specs=pl.BlockSpec(memory_space=pltpu.VMEM),
+        scratch_shapes=[
+            pltpu.VMEM((depth, columns), jnp.bfloat16),
+            pltpu.VMEM((CHUNKS, rows, wide), jnp.float32),
+            pltpu.VMEM((CHUNKS, rows, wide), jnp.float32),
+            pltpu.VMEM((rounds, CHUNKS, rows, wide), jnp.bfloat16),
+            pltpu.VMEM((rounds, CHUNKS, rows, wide), jnp.bfloat16),
+            pltpu.SemaphoreType.DMA((2, CHUNKS)),
+            pltpu.SemaphoreType.DMA((CHUNKS,)),
+            pltpu.SemaphoreType.DMA((CHUNKS,)),
+            pltpu.SemaphoreType.DMA((rounds, CHUNKS)),
+            pltpu.SemaphoreType.DMA((rounds, CHUNKS)),
+            pltpu.SemaphoreType.DMA((CHUNKS,)),
+            pltpu.SemaphoreType.DMA((CHUNKS,)),
+        ],
+        compiler_params=pltpu.CompilerParams(
+            collective_id=0, has_side_effects=True, vmem_limit_bytes=32 * 2**20
+        ),
+        cost_estimate=pl.CostEstimate(
+            flops=2 * rows * depth * columns,
+            bytes_accessed=2 * depth * columns + 4 * rows * columns,
+            transcendentals=0,
+        ),
+    )(gated, out_weight)
 
 
 def on_device(
@@ -66,8 +226,7 @@
     convolved = lax.all_to_all(convolved, "seq", 0, 0, tiled=True)
     convolved = convolved.transpose(1, 0, 2).reshape(shard_len, width).astype(jnp.float32)
     gated = (shape_stream(0) * (convolved + skip_gain * source)).astype(jnp.bfloat16)
-    terms = jnp.dot(gated, out_weight, preferred_element_type=jnp.float32)
-    return lax.psum(terms.astype(jnp.bfloat16), "chan")
+    return project(gated, out_weight)
 
 
 def solution(mesh):

time: 151 us -> 110 us (0.73)
  the two profiles are of different devices: /device:TPU:29 before, /device:TPU:0 now
where the time goes in v2:
time: 110 us
  Pallas kernels  31.7 us (29%)
  blocking collectives  30.2 us (27%)
  waiting for transfers between devices  13.9 us (13%)
  matrix products  12.5 us (11%)
  local copies, waits for them, and re-layouts  9.28 us (8%)
  starting transfers between devices  8.41 us (8%)
  other arithmetic  3.28 us (3%)
    pallas_call x1, Pallas kernels, project(): pl.pallas_call(functools.partial(project_kernel, rounds), out_shape=jax.S...  31.7 us
    all_to_all x1, blocking collectives, on_device(): lax.all_to_all(fields, 'seq', 0, 0, tiled=True).reshape(seq_len, 2 * part)  30.2 us
    all_to_all x1, waiting for transfers between devices, on_device(): convolved = lax.all_to_all(convolved, 'seq', 0, 0, tiled=True)  13.9 us
    dot_general x1, matrix products, on_device(): spec = jnp.dot(matrix, fields, preferred_element_type=jnp.float32)  10.2 us
    unnamed x19, local copies, waits for them, and re-layouts  4.9 us
    ppermute x1, starting transfers between devices, from_behind(): return lax.ppermute(array, axis, pairs)  4.87 us
    all_to_all x1, starting transfers between devices, on_device(): convolved = lax.all_to_all(convolved, 'seq', 0, 0, tiled=True)  3.54 us
    dot_general x1, matrix products, on_device(): lax.dot_general(matrix, prod.astype(jnp.bfloat16), (((0,), (0,)), ((), ()...  2.36 us
  transfers between devices with their start and end apart: 2, of which 1 were waited for; matrix products, arithmetic and copies ran while one was open for 2% of the time, Pallas kernels for 0%

profile of v2, /device:TPU:0, one launch (start us, length us, event | category | flops | bytes accessed | tf_op | source)
XLA Modules:
  0.0 109.6 jit_solution(13900553123421538508)
XLA Ops:
  0.0 0.8 slice_bitcast_fusion.5
  0.8 0.7 slice_bitcast_fusion.3
  1.6 4.9 %collective-permute-start = (bf16[3,2,1024]{2,1,0:T(2,128)(2,1)S(1)}, bf16[3,2,1024]{2,1,0:T(2,128)(2,1)S(1)}, u32[]{:S(2)}, u32[]{:S(2)}) collective-permute-start(bf16[3,2,1024]{2,1,0:T(2,128)(2,1)S(1)} %pad_maximum_fusion.1), channel_id=1, source_target_pairs={{0,4},{4,8},{8,12},{12,16},{16,20},{20,24},{24,28},{1,5},{5,9},{9,... | collective-permute-start | bytes 36872 | tf_op jit(solution)/shard_map/ppermute | solution.py:25
  6.4 0.9 fusion.17
  7.4 1.4 %convert_element_type.40 = bf16[256,1024]{1,0:T(8,128)(2,1)S(1)} convert(f32[256,1024]{1,0:T(8,128)} %param.13) | non-fusion elementwise | flops 262144 | bytes 1572864 | tf_op jit(solution)/shard_map/convert_element_type | solution.py:210
  8.7 0.2 copy.17
  9.0 0.1 maximum_convert_fusion.1
  9.2 0.1 maximum_convert_fusion.2
  9.3 0.7 fusion.15
  10.0 0.2 copy.22
  10.3 30.2 %all_to_all.10 = bf16[8,256,256]{1,2,0:T(8,128)(2,1)S(1)} all-to-all(bf16[8,256,256]{1,2,0:T(8,128)(2,1)S(1)} %bitcast.45), channel_id=1, replica_groups=mesh['seq'=8,'chan'=4] {'seq'}, dimensions={0} | all-to-all | bytes 2097152 | tf_op jit(solution)/shard_map/all_to_all | solution.py:213
  40.5 0.5 copy.19
  41.1 10.2 %fusion.18 = f32[4096,256]{1,0:T(8,128)S(1)} fusion(bf16[4096,2048]{1,0:T(8,128)(2,1)} %constant.4.clone, bf16[2048,256]{1,0:T(8,128)(2,1)S(1)} %bitcast.48), kind=kOutput, calls=%fused_computation.42 | convolution fusion | flops 4294967296 | bytes 22020096 | tf_op jit(solution)/shard_map/dot_general | solution.py:214
  51.3 0.2 multiply_subtract_fusion
  51.5 0.1 slice-done.3
  51.7 2.4 %fusion = bf16[2048,128]{0,1:T(8,128)(2,1)S(1)} fusion(bf16[4096,2048]{1,0:T(8,128)(2,1)S(1)} %bitcast.44, f32[2048,128]{1,0:T(8,128)S(1)} %get-tuple-element.8, f32[2048,128]{1,0:T(8,128)S(1)} %get-tuple-element.7), kind=kOutput, calls=%fused_computation.1 | convolution fusion | flops 2149318656 | bytes 19398656 | tf_op jit(solution)/shard_map/dot_general | solution.py:219
  54.1 1.0 copy.23
  55.1 3.5 %all-to-all-start.1 = ((bf16[8,256,128]{2,1,0:T(8,128)(2,1)}), bf16[8,256,128]{2,1,0:T(8,128)(2,1)S(1)}, u32[]{:S(2)}, u32[]{:S(2)}) async-start(bf16[8,256,128]{2,1,0:T(8,128)(2,1)} %bitcast.21), calls=%async_computation.1 | async-start | bytes 1048576 | tf_op jit(solution)/shard_map/all_to_all | solution.py:226
  58.6 0.1 maximum_convert_fusion
  58.8 13.9 %all-to-all-done.1 = bf16[8,256,128]{2,1,0:T(8,128)(2,1)S(1)} async-done(((bf16[8,256,128]{2,1,0:T(8,128)(2,1)}), bf16[8,256,128]{2,1,0:T(8,128)(2,1)S(1)}, u32[]{:S(2)}, u32[]{:S(2)}) %all-to-all-start.1) | async-done | bytes 524320 | tf_op jit(solution)/shard_map/all_to_all | solution.py:226
  72.7 0.5 fusion.4.gated_ref
  73.1 3.4 %copy-done = bf16[1024,4096]{1,0:T(8,128)(2,1)S(1)} copy-done((bf16[1024,4096]{1,0:T(8,128)(2,1)S(1)}, bf16[1024,4096]{1,0:T(8,128)(2,1)}, u32[]{:S(2)}) %copy-start) | copy-done | bytes 8388632
  76.5 31.7 %shard_map.82 = bf16[256,4096]{1,0:T(8,128)(2,1)S(1)} custom-call(bf16[256,1024]{1,0:T(8,128)(2,1)S(1)} %fusion.4.gated_ref, bf16[1024,4096]{1,0:T(8,128)(2,1)S(1)} %copy-done), custom_call_target="tpu_custom_call" | custom-call | flops 2147483648 | bytes 12582912 | tf_op jit(solution)/shard_map/pallas_call | solution.py:154
  108.2 1.3 %copy.27 = bf16[256,4096]{1,0:T(8,128)(2,1)} copy(bf16[256,4096]{1,0:T(8,128)(2,1)S(1)} %shard_map.82) | data formatting | bytes 4194304
  (21 shorter events, 0.2 us)
Async XLA Ops:
  0.0 9.0 %copy-start.1 = (bf16[256,1024]{1,0:T(8,128)(2,1)S(1)}, bf16[256,1024]{1,0:T(8,128)(2,1)}, u32[]{:S(2)}) copy-start(bf16[256,1024]{1,0:T(8,128)(2,1)} %param.9) | copy-start | bytes 1572868
  1.6 7.4 %collective-permute-start = (bf16[3,2,1024]{2,1,0:T(2,128)(2,1)S(1)}, bf16[3,2,1024]{2,1,0:T(2,128)(2,1)S(1)}, u32[]{:S(2)}, u32[]{:S(2)}) collective-permute-start(bf16[3,2,1024]{2,1,0:T(2,128)(2,1)S(1)} %pad_maximum_fusion.1), channel_id=1, source_target_pairs={{0,4},{4,8},{8,12},{12,16},{16,20},{20,24},{24,28},{1,5},{5,9},{9,... | collective-permute-start | bytes 36872 | tf_op jit(solution)/shard_map/ppermute | solution.py:25
  7.4 1.8 %copy-start.2 = (bf16[256,1024]{1,0:T(8,128)(2,1)S(1)}, bf16[256,1024]{1,0:T(8,128)(2,1)}, u32[]{:S(2)}) copy-start(bf16[256,1024]{1,0:T(8,128)(2,1)} %param.10) | copy-start | bytes 1572868
  41.0 10.5 %slice-start = ((s8[16777216]{0:T(1024)(128)(4,1)}), s8[4194304]{0:T(1024)(128)(4,1)S(1)}, s32[]{:S(2)}) async-start(s8[16777216]{0:T(1024)(128)(4,1)} %bitcast.43), calls=%async_computation.2 | async-start | bytes 8388608
  41.1 10.5 %slice-start.1 = ((s8[16777216]{0:T(1024)(128)(4,1)}), s8[4194304]{0:T(1024)(128)(4,1)S(1)}, s32[]{:S(2)}) async-start(s8[16777216]{0:T(1024)(128)(4,1)} %bitcast.43), calls=%async_computation.3 | async-start | bytes 8388608
  41.1 10.5 %slice-start.2 = ((s8[16777216]{0:T(1024)(128)(4,1)}), s8[4194304]{0:T(1024)(128)(4,1)S(1)}, s32[]{:S(2)}) async-start(s8[16777216]{0:T(1024)(128)(4,1)} %bitcast.43), calls=%async_computation.4 | async-start | bytes 8388608
  41.1 10.6 %slice-start.3 = ((s8[16777216]{0:T(1024)(128)(4,1)}), s8[4194304]{0:T(1024)(128)(4,1)S(1)}, s32[]{:S(2)}) async-start(s8[16777216]{0:T(1024)(128)(4,1)} %bitcast.43), calls=%async_computation.5 | async-start | bytes 8388608
  54.0 4.6 %copy-start.3 = (bf16[256,1024]{1,0:T(8,128)(2,1)S(1)}, bf16[256,1024]{1,0:T(8,128)(2,1)}, u32[]{:S(2)}) copy-start(bf16[256,1024]{1,0:T(8,128)(2,1)} %param.8) | copy-start | bytes 1572868
  54.1 18.6 %copy-start.4 = (f32[1024]{0:T(1024)S(1)}, f32[1024]{0:T(1024)}, u32[]{:S(2)}) copy-start(f32[1024]{0:T(1024)} %param.12) | copy-start | bytes 12292
  55.1 17.6 %all-to-all-start.1 = ((bf16[8,256,128]{2,1,0:T(8,128)(2,1)}), bf16[8,256,128]{2,1,0:T(8,128)(2,1)S(1)}, u32[]{:S(2)}, u32[]{:S(2)}) async-start(bf16[8,256,128]{2,1,0:T(8,128)(2,1)} %bitcast.21), calls=%async_computation.1 | async-start | bytes 1048576 | tf_op jit(solution)/shard_map/all_to_all | solution.py:226
  73.1 3.4 %copy-start = (bf16[1024,4096]{1,0:T(8,128)(2,1)S(1)}, bf16[1024,4096]{1,0:T(8,128)(2,1)}, u32[]{:S(2)}) copy-start(bf16[1024,4096]{1,0:T(8,128)(2,1)} %weight_ref.1) | copy-start | bytes 25165828

commit v3 on v2

--- a/solution.py
+++ b/solution.py
@@ -10,13 +10,19 @@
 from jax.sharding import PartitionSpec as P
 
 
+FREQS = 256
+SLOTS = 4
+LANES = 128
+
+
 def transform(seq_len):
     period = 4 * seq_len
-    freq = 2 * np.arange(seq_len, dtype=np.int64) + 1
+    freq = 2 * np.arange(seq_len // 2, dtype=np.int64) + 1
     turns = freq[:, None] * np.arange(seq_len, dtype=np.int64)[None, :] % period
     angle = np.arange(period) * (2.0 * np.pi / period)
     table = np.stack([np.cos(angle), np.sin(angle)]).astype(ml_dtypes.bfloat16)
-    return table[:, turns].reshape(2 * seq_len, seq_len)
+    groups = table[:, turns].reshape(2, -1, FREQS, seq_len)
+    return groups.transpose(1, 0, 2, 3).reshape(-1, 2 * FREQS, seq_len)
 
 
 def from_behind(array, axis, by):
@@ -171,7 +177,7 @@
             pltpu.SemaphoreType.DMA((CHUNKS,)),
         ],
         compiler_params=pltpu.CompilerParams(
-            collective_id=0, has_side_effects=True, vmem_limit_bytes=32 * 2**20
+            collective_id=1, has_side_effects=True, vmem_limit_bytes=32 * 2**20
         ),
         cost_estimate=pl.CostEstimate(
             flops=2 * rows * depth * columns,
@@ -179,6 +185,160 @@
             transcendentals=0,
         ),
     )(gated, out_weight)
+
+
+def convolve_kernel(
+    fields_ref,
+    matrix_ref,
+    out_ref,
+    fields,
+    data,
+    bank,
+    total,
+    back,
+    bank_sem,
+    send_sem,
+    recv_sem,
+    back_send_sem,
+    back_recv_sem,
+):
+    count, shard_len, _ = fields_ref.shape
+    lanes = out_ref.shape[2]
+    groups, _, seq_len = matrix_ref.shape
+    slots = bank.shape[0]
+    me = lax.axis_index("seq")
+
+    def bank_copy(group):
+        slot = lax.rem(group, slots)
+        return pltpu.make_async_copy(matrix_ref.at[group], bank.at[slot], bank_sem.at[slot])
+
+    def there(hop):
+        peer = lax.rem(me + hop, count)
+        return pltpu.make_async_remote_copy(
+            src_ref=fields_ref.at[peer],
+            dst_ref=fields.at[me],
+            send_sem=send_sem.at[hop],
+            recv_sem=recv_sem.at[hop],
+            device_id={"seq": peer},
+            device_id_type=MESH,
+        )
+
+    def again(hop):
+        peer = lax.rem(me + hop, count)
+        return pltpu.make_async_remote_copy(
+            src_ref=back.at[peer],
+            dst_ref=out_ref.at[me],
+            send_sem=back_send_sem.at[hop],
+            recv_sem=back_recv_sem.at[hop],
+            device_id={"seq": peer},
+            device_id_type=MESH,
+        )
+
+    barrier = pltpu.get_barrier_semaphore()
+
+    @pl.loop(1, count)
+    def _(hop):
+        peer = lax.rem(me + hop, count)
+        pl.semaphore_signal(barrier, inc=1, device_id={"seq": peer}, device_id_type=MESH)
+
+    pl.semaphore_wait(barrier, count - 1)
+
+    @pl.loop(1, count)
+    def _(hop):
+        there(hop).start()
+
+    @pl.loop(0, slots)
+    def _(group):
+        bank_copy(group).start()
+
+    fields[me] = fields_ref[me]
+    total[...] = jnp.zeros_like(total)
+
+    @pl.loop(1, count)
+    def _(hop):
+        there(hop).wait_recv()
+
+    def signs(shape, axis):
+        return (1 - 2 * lax.rem(lax.broadcasted_iota(jnp.int32, shape, axis), 2)).astype(
+            jnp.float32
+        )
+
+    @pl.loop(0, count)
+    def _(shard):
+        rows = pl.ds(pl.multiple_of(shard * shard_len, shard_len), shard_len)
+        plain = fields[shard]
+        data[rows, : 2 * lanes] = plain
+        flipped = plain.astype(jnp.float32) * signs(plain.shape, 0)
+        data[rows, 2 * lanes :] = flipped.astype(jnp.bfloat16)
+
+    @pl.loop(0, groups)
+    def _(group):
+        bank_copy(group).wait()
+        slot = lax.rem(group, slots)
+        spec = jnp.dot(bank[slot], data[...], preferred_element_type=jnp.float32)
+
+        def product(first):
+            a, b = (spec[:FREQS, first + x : first + x + lanes] for x in (0, lanes))
+            c, d = (spec[FREQS:, first + x : first + x + lanes] for x in (0, lanes))
+            return jnp.concatenate([a * b - c * d, a * d + c * b]) * (1.0 / seq_len)
+
+        prod = jnp.concatenate([product(0).T, product(2 * lanes).T]).astype(jnp.bfloat16)
+        total[...] += jnp.dot(prod, bank[slot], preferred_element_type=jnp.float32)
+
+        @pl.when(group + slots < groups)
+        def _():
+            bank_copy(group + slots).start()
+
+    def block(peer):
+        columns = pl.ds(pl.multiple_of(peer * shard_len, shard_len), shard_len)
+        plain, flipped = total[:lanes, columns], total[lanes:, columns]
+        return (plain + flipped * signs(plain.shape, 1)).T.astype(jnp.bfloat16)
+
+    @pl.loop(1, count)
+    def _(hop):
+        peer = lax.rem(me + hop, count)
+        back[peer] = block(peer)
+        again(hop).start()
+
+    out_ref[me] = block(me)
+
+    @pl.loop(1, count)
+    def _(hop):
+        there(hop).wait_send()
+        again(hop).wait()
+
+
+def convolve(fields, matrix):
+    count, shard_len, wide = fields.shape
+    groups, rows, seq_len = matrix.shape
+    slots = min(SLOTS, groups)
+    lanes = wide // 2
+    return pl.pallas_call(
+        convolve_kernel,
+        out_shape=jax.ShapeDtypeStruct((count, shard_len, lanes), jnp.bfloat16),
+        in_specs=[pl.BlockSpec(memory_space=pltpu.VMEM), pl.BlockSpec(memory_space=pl.ANY)],
+        out_specs=pl.BlockSpec(memory_space=pltpu.VMEM),
+        scratch_shapes=[
+            pltpu.VMEM((count, shard_len, wide), jnp.bfloat16),
+            pltpu.VMEM((seq_len, 2 * wide), jnp.bfloat16),
+            pltpu.VMEM((slots, rows, seq_len), jnp.bfloat16),
+            pltpu.VMEM((wide, seq_len), jnp.float32),
+            pltpu.VMEM((count, shard_len, lanes), jnp.bfloat16),
+            pltpu.SemaphoreType.DMA((slots,)),
+            pltpu.SemaphoreType.DMA((count,)),
+            pltpu.SemaphoreType.DMA((count,)),
+            pltpu.SemaphoreType.DMA((count,)),
+            pltpu.SemaphoreType.DMA((count,)),
+        ],
+        compiler_params=pltpu.CompilerParams(
+            collective_id=0, has_side_effects=True, vmem_limit_bytes=52 * 2**20
+        ),
+        cost_estimate=pl.CostEstimate(
+            flops=12 * groups * rows * seq_len * lanes,
+            bytes_accessed=2 * groups * rows * seq_len,
+            transcendentals=0,
+        ),
+    )(fields, matrix)
 
 
 def on_device(
@@ -193,7 +353,6 @@
 ):
     shard_len, width = query_projected.shape
     seq_count = lax.axis_size("seq")
-    seq_len = seq_count * shard_len
     part = width // seq_count
     streams = [query_projected, key_stream, value_stream]
     rims = from_behind(jnp.stack([x[-2:] for x in streams]), "seq", 1)
@@ -207,23 +366,12 @@
         )
 
     source = shape_stream(1) * shape_stream(2)
+    lanes = -(-part // LANES) * LANES
     fields = jnp.stack([source.astype(jnp.bfloat16), long_filter.astype(jnp.bfloat16)])
     fields = fields.reshape(2, shard_len, seq_count, part).transpose(2, 1, 0, 3)
-    fields = fields.reshape(seq_count, shard_len, 2 * part)
-    fields = lax.all_to_all(fields, "seq", 0, 0, tiled=True).reshape(seq_len, 2 * part)
-    spec = jnp.dot(matrix, fields, preferred_element_type=jnp.float32)
-    real, imag = spec[:seq_len], spec[seq_len:]
-    a, b = real[:, :part], real[:, part:]
-    c, d = imag[:, :part], imag[:, part:]
-    prod = jnp.concatenate([a * b - c * d, a * d + c * b]) * (1.0 / seq_len)
-    convolved = lax.dot_general(
-        matrix,
-        prod.astype(jnp.bfloat16),
-        (((0,), (0,)), ((), ())),
-        preferred_element_type=jnp.float32,
-    ).astype(jnp.bfloat16)
-    convolved = convolved.reshape(seq_count, shard_len, part)
-    convolved = lax.all_to_all(convolved, "seq", 0, 0, tiled=True)
+    fields = jnp.pad(fields, ((0, 0), (0, 0), (0, 0), (0, lanes - part)))
+    fields = fields.reshape(seq_count, shard_len, 2 * lanes)
+    convolved = convolve(fields, matrix)[:, :, :part]
     convolved = convolved.transpose(1, 0, 2).reshape(shard_len, width).astype(jnp.float32)
     gated = (shape_stream(0) * (convolved + skip_gain * source)).astype(jnp.bfloat16)
     return project(gated, out_weight)
@@ -234,7 +382,7 @@
         on_device,
         mesh=mesh,
         in_specs=(
-            P(None, None),
+            P(None, None, None),
             P("seq", "chan"),
             P("seq", "chan"),
             P("seq", "chan"),

time: 110 us -> 91.5 us (0.83)
  the two profiles are of different devices: /device:TPU:0 before, /device:TPU:29 now
where the time goes in v3:
time: 91.5 us; the launch traced here: 91 us
  Pallas kernels  78.5 us (86%)
  local copies, waits for them, and re-layouts  5.17 us (6%)
  other arithmetic  3.99 us (4%)
  waiting for transfers between devices  1.67 us (2%)
  starting transfers between devices  1.42 us (2%)
    pallas_call x1, Pallas kernels, convolve(): pl.pallas_call(convolve_kernel, out_shape=jax.ShapeDtypeStruct((count, sh...  46.5 us
    pallas_call x1, Pallas kernels, project(): pl.pallas_call(functools.partial(project_kernel, rounds), out_shape=jax.S...  32.1 us
    unnamed x3, other arithmetic  2.96 us
    unnamed x19, local copies, waits for them, and re-layouts  1.87 us
  transfers between devices with their start and end apart: 1, of which 1 were waited for; matrix products, arithmetic and copies ran while one was open for 2% of the time, Pallas kernels for 0%

profile of v3, /device:TPU:29, one launch (start us, length us, event | category | flops | bytes accessed | tf_op | source)
XLA Modules:
  0.0 91.0 jit_solution(4560817105325967566)
XLA Ops:
  0.0 0.7 slice_bitcast_fusion.5
  0.7 0.7 slice_bitcast_fusion.3
  1.5 0.0 copy-start.1
  1.5 1.4 %collective-permute-start = (bf16[3,2,1024]{2,1,0:T(2,128)(2,1)S(1)}, bf16[3,2,1024]{2,1,0:T(2,128)(2,1)S(1)}, u32[]{:S(2)}, u32[]{:S(2)}) collective-permute-start(bf16[3,2,1024]{2,1,0:T(2,128)(2,1)S(1)} %pad_maximum_fusion), channel_id=1, source_target_pairs={{0,4},{4,8},{8,12},{12,16},{16,20},{20,24},{24,28},{1,5},{5,9},{9,... | collective-permute-start | bytes 36872 | tf_op jit(solution)/shard_map/ppermute | solution.py:31
  3.0 1.3 %convert_bitcast_fusion.1 = bf16[32,8,8,128]{3,1,2,0:T(8,128)(2,1)S(1)} fusion(f32[256,1024]{1,0:T(8,128)} %param.13), kind=kLoop, calls=%fused_computation.24 | loop fusion | flops 262144 | bytes 1572864
  4.3 0.0 copy-start.2
  4.3 0.1 copy.13
  4.4 1.7 %collective-permute-done = bf16[3,2,1024]{2,1,0:T(2,128)(2,1)S(1)} collective-permute-done((bf16[3,2,1024]{2,1,0:T(2,128)(2,1)S(1)}, bf16[3,2,1024]{2,1,0:T(2,128)(2,1)S(1)}, u32[]{:S(2)}, u32[]{:S(2)}) %collective-permute-start) | collective-permute-done | bytes 12320 | tf_op jit(solution)/shard_map/ppermute | solution.py:31
  6.1 0.1 maximum_convert_fusion.1
  6.3 0.1 maximum_convert_fusion.2
  6.4 1.7 %convert_bitcast_fusion.2 = (bf16[32,8,8,128]{3,1,2,0:T(8,128)(2,1)S(1)}, f32[256,1024]{1,0:T(8,128)}) fusion(f32[258,1024]{1,0:T(8,128)S(1)} %maximum_convert_fusion.2, f32[1024]{0:T(1024)S(1)} %bitcast.52, f32[1024]{0:T(1024)S(1)} %bitcast.53, f32[1024]{0:T(1024)S(1)} %bitcast.48, f32[258,1024]{1,0:T(8,128)S(1)} %maximum_convert_fusion.1, ...), kind=kLoop, calls=%fused_computation.25 | loop fusion | flops 3145728 | bytes 7888896
  8.1 0.1 copy.12
  8.2 0.1 maximum_bitcast_fusion
  8.3 1.1 %copy.9 = bf16[8,256,2,128]{3,2,1,0:T(2,128)(2,1)S(1)} copy(bf16[8,256,2,128]{3,0,1,2:T(8,128)(2,1)S(1)} %maximum_bitcast_fusion) | data formatting | bytes 2097152 | tf_op jit(solution)/shard_map/transpose | solution.py:371
  9.4 0.0 copy-start.3
  9.4 0.7 reshape.21.fields_ref
  10.1 0.3 copy-done.3
  10.4 0.1 maximum_convert_fusion
  10.6 0.0 copy-start
  10.6 0.0 slice-start.1
  10.6 46.5 %shard_map.82 = bf16[8,256,128]{2,1,0:T(8,128)(2,1)S(1)} custom-call(bf16[8,256,256]{2,1,0:T(8,128)(2,1)S(1)} %reshape.21.fields_ref, bf16[4,512,2048]{2,1,0:T(8,128)(2,1)} %constant.1.clone.matrix_ref), custom_call_target="tpu_custom_call" | custom-call | flops 6442450944 | bytes 8388608 | tf_op jit(solution)/shard_map/pallas_call | solution.py:316
  57.2 0.5 fusion.1.gated_ref
  57.7 32.1 %shard_map.83 = bf16[256,4096]{1,0:T(8,128)(2,1)S(1)} custom-call(bf16[256,1024]{1,0:T(8,128)(2,1)S(1)} %fusion.1.gated_ref, bf16[1024,4096]{1,0:T(8,128)(2,1)S(1)} %bitcast.42), custom_call_target="tpu_custom_call" | custom-call | flops 2147483648 | bytes 12582912 | tf_op jit(solution)/shard_map/pallas_call | solution.py:160
  89.7 1.3 %copy.16 = bf16[256,4096]{1,0:T(8,128)(2,1)} copy(bf16[256,4096]{1,0:T(8,128)(2,1)S(1)} %shard_map.83) | data formatting | bytes 4194304
  (14 shorter events, 0.1 us)
Async XLA Ops:
  0.0 4.3 %copy-start.4 = (f32[3,3,1024]{2,1,0:T(4,128)S(1)}, f32[3,3,1024]{2,1,0:T(4,128)}, u32[]{:S(2)}) copy-start(f32[3,3,1024]{2,1,0:T(4,128)} %param.11) | copy-start | bytes 110596
  1.5 4.6 %copy-start.1 = (bf16[256,1024]{1,0:T(8,128)(2,1)S(1)}, bf16[256,1024]{1,0:T(8,128)(2,1)}, u32[]{:S(2)}) copy-start(bf16[256,1024]{1,0:T(8,128)(2,1)} %param.9) | copy-start | bytes 1572868
  1.5 4.6 %collective-permute-start = (bf16[3,2,1024]{2,1,0:T(2,128)(2,1)S(1)}, bf16[3,2,1024]{2,1,0:T(2,128)(2,1)S(1)}, u32[]{:S(2)}, u32[]{:S(2)}) collective-permute-start(bf16[3,2,1024]{2,1,0:T(2,128)(2,1)S(1)} %pad_maximum_fusion), channel_id=1, source_target_pairs={{0,4},{4,8},{8,12},{12,16},{16,20},{20,24},{24,28},{1,5},{5,9},{9,... | collective-permute-start | bytes 36872 | tf_op jit(solution)/shard_map/ppermute | solution.py:31
  4.3 2.0 %copy-start.2 = (bf16[256,1024]{1,0:T(8,128)(2,1)S(1)}, bf16[256,1024]{1,0:T(8,128)(2,1)}, u32[]{:S(2)}) copy-start(bf16[256,1024]{1,0:T(8,128)(2,1)} %param.10) | copy-start | bytes 1572868
  9.4 1.0 %copy-start.3 = (bf16[256,1024]{1,0:T(8,128)(2,1)S(1)}, bf16[256,1024]{1,0:T(8,128)(2,1)}, u32[]{:S(2)}) copy-start(bf16[256,1024]{1,0:T(8,128)(2,1)} %param.8) | copy-start | bytes 1572868
  10.4 47.2 %slice-start = ((s8[8388608]{0:T(1024)(128)(4,1)}), s8[4194304]{0:T(1024)(128)(4,1)S(1)}, s32[]{:S(2)}) async-start(s8[8388608]{0:T(1024)(128)(4,1)} %bitcast.41), calls=%async_computation | async-start | bytes 8388608
  10.6 46.5 %copy-start = (f32[256,1024]{1,0:T(8,128)S(1)}, f32[256,1024]{1,0:T(8,128)}, u32[]{:S(2)}) copy-start(f32[256,1024]{1,0:T(8,128)} %get-tuple-element.6) | copy-start | bytes 3145732
  10.6 46.5 %copy-start.5 = (f32[1024]{0:T(1024)S(1)}, f32[1024]{0:T(1024)}, u32[]{:S(2)}) copy-start(f32[1024]{0:T(1024)} %param.12) | copy-start | bytes 12292
  10.6 47.0 %slice-start.1 = ((s8[8388608]{0:T(1024)(128)(4,1)}), s8[4194304]{0:T(1024)(128)(4,1)S(1)}, s32[]{:S(2)}) async-start(s8[8388608]{0:T(1024)(128)(4,1)} %bitcast.41), calls=%async_computation.1 | async-start | bytes 8388608

commit v4 on v2

--- a/solution.py
+++ b/solution.py
@@ -10,19 +10,19 @@
 from jax.sharding import PartitionSpec as P
 
 
+FREQS = 256
+RIM = 16
+LANES = 128
+
+
 def transform(seq_len):
     period = 4 * seq_len
-    freq = 2 * np.arange(seq_len, dtype=np.int64) + 1
+    freq = 2 * np.arange(seq_len // 2, dtype=np.int64) + 1
     turns = freq[:, None] * np.arange(seq_len, dtype=np.int64)[None, :] % period
     angle = np.arange(period) * (2.0 * np.pi / period)
     table = np.stack([np.cos(angle), np.sin(angle)]).astype(ml_dtypes.bfloat16)
-    return table[:, turns].reshape(2 * seq_len, seq_len)
-
-
-def from_behind(array, axis, by):
-    peers = lax.axis_size(axis)
-    pairs = [(i, i + by) for i in range(peers) if 0 <= i + by < peers]
-    return lax.ppermute(array, axis, pairs)
+    groups = table[:, turns].reshape(2, -1, FREQS, seq_len)
+    return groups.transpose(1, 0, 2, 3).reshape(-1, 2 * FREQS, seq_len)
 
 
 CHUNKS = 4
@@ -171,7 +171,7 @@
             pltpu.SemaphoreType.DMA((CHUNKS,)),
         ],
         compiler_params=pltpu.CompilerParams(
-            collective_id=0, has_side_effects=True, vmem_limit_bytes=32 * 2**20
+            collective_id=1, has_side_effects=True, vmem_limit_bytes=32 * 2**20
         ),
         cost_estimate=pl.CostEstimate(
             flops=2 * rows * depth * columns,
@@ -179,6 +179,205 @@
             transcendentals=0,
         ),
     )(gated, out_weight)
+
+
+def gate_kernel(
+    query_ref,
+    key_ref,
+    value_ref,
+    taps_ref,
+    skip_ref,
+    filter_ref,
+    matrix_ref,
+    gated_ref,
+    rim,
+    extended,
+    query,
+    source,
+    outgoing,
+    incoming,
+    data,
+    bank,
+    filter_spec,
+    total,
+    back,
+    convolved,
+    bank_sem,
+    rim_send_sem,
+    rim_recv_sem,
+    send_sem,
+    recv_sem,
+    back_send_sem,
+    back_recv_sem,
+):
+    _, count, shard_len, lanes = outgoing.shape
+    groups, _, seq_len = matrix_ref.shape
+    part = query_ref.shape[1] // count
+    me = lax.axis_index("seq")
+    streams = (query_ref, key_ref, value_ref)
+
+    def bank_copy(group):
+        return pltpu.make_async_copy(matrix_ref.at[group], bank.at[group], bank_sem.at[group])
+
+    def rim_copy(index):
+        return pltpu.make_async_remote_copy(
+            src_ref=streams[index].at[pl.ds(shard_len - RIM, RIM)],
+            dst_ref=rim.at[index],
+            send_sem=rim_send_sem.at[index],
+            recv_sem=rim_recv_sem.at[index],
+            device_id={"seq": lax.rem(me + 1, count)},
+            device_id_type=MESH,
+        )
+
+    def there(field, hop):
+        peer = lax.rem(me + hop, count)
+        return pltpu.make_async_remote_copy(
+            src_ref=outgoing.at[field, peer],
+            dst_ref=incoming.at[field, me],
+            send_sem=send_sem.at[field, hop],
+            recv_sem=recv_sem.at[field, hop],
+            device_id={"seq": peer},
+            device_id_type=MESH,
+        )
+
+    def again(hop):
+        peer = lax.rem(me + hop, count)
+        return pltpu.make_async_remote_copy(
+            src_ref=back.at[peer],
+            dst_ref=convolved.at[me],
+            send_sem=back_send_sem.at[hop],
+            recv_sem=back_recv_sem.at[hop],
+            device_id={"seq": peer},
+            device_id_type=MESH,
+        )
+
+    def split(field, ref):
+        if part < lanes:
+            outgoing[field] = jnp.zeros(outgoing.shape[1:], outgoing.dtype)
+        for peer in range(count):
+            columns = ref[:, peer * part : (peer + 1) * part]
+            outgoing[field, peer, :, :part] = columns.astype(jnp.bfloat16)
+
+    def send(field):
+        @pl.loop(1, count)
+        def _(hop):
+            there(field, hop).start()
+
+        incoming[field, me] = outgoing[field, me]
+
+    def signs(shape, axis):
+        return (1 - 2 * lax.rem(lax.broadcasted_iota(jnp.int32, shape, axis), 2)).astype(
+            jnp.float32
+        )
+
+    def receive(field):
+        @pl.loop(1, count)
+        def _(hop):
+            there(field, hop).wait_recv()
+
+        @pl.loop(0, count)
+        def _(shard):
+            rows = pl.ds(pl.multiple_of(shard * shard_len, shard_len), shard_len)
+            plain = incoming[field, shard]
+            data[rows, :lanes] = plain
+            flipped = plain.astype(jnp.float32) * signs(plain.shape, 0)
+            data[rows, lanes:] = flipped.astype(jnp.bfloat16)
+
+    def shaped(index):
+        extended[:8] = rim[index].astype(jnp.float32)[RIM - 8 :]
+        extended[8:] = streams[index][...].astype(jnp.float32)
+        result = taps_ref[0, index : index + 1] * extended[8:]
+        for tap in (1, 2):
+            rows = extended[8 - tap : 8 - tap + shard_len]
+            result = result + taps_ref[tap, index : index + 1] * rows
+        return result
+
+    barrier = pltpu.get_barrier_semaphore()
+
+    @pl.loop(1, count)
+    def _(hop):
+        peer = lax.rem(me + hop, count)
+        pl.semaphore_signal(barrier, inc=1, device_id={"seq": peer}, device_id_type=MESH)
+
+    split(0, filter_ref)
+    pl.semaphore_wait(barrier, count - 1)
+
+    @pl.when(me < count - 1)
+    def _():
+        for index in range(3):
+            rim_copy(index).start()
+
+    send(0)
+
+    @pl.loop(0, groups)
+    def _(group):
+        bank_copy(group).start()
+
+    @pl.when(me == 0)
+    def _():
+        rim[...] = jnp.zeros_like(rim)
+
+    @pl.when(me > 0)
+    def _():
+        for index in range(3):
+            rim_copy(index).wait_recv()
+
+    source[...] = shaped(1)
+    source[...] = source[...] * shaped(2)
+    split(1, source)
+    send(1)
+    query[...] = shaped(0)
+    total[...] = jnp.zeros_like(total)
+
+    receive(0)
+
+    @pl.loop(0, groups)
+    def _(group):
+        bank_copy(group).wait()
+        filter_spec[group] = jnp.dot(
+            bank[group], data[...], preferred_element_type=jnp.float32
+        )
+
+    receive(1)
+
+    @pl.loop(0, groups)
+    def _(group):
+        spec = jnp.dot(bank[group], data[...], preferred_element_type=jnp.float32)
+        a, c = spec[:FREQS], spec[FREQS:]
+        b, d = filter_spec[group, :FREQS], filter_spec[group, FREQS:]
+        prod = jnp.concatenate([a * b - c * d, a * d + c * b]) * (1.0 / seq_len)
+        prod = jnp.concatenate([prod[:, :lanes].T, prod[:, lanes:].T]).astype(jnp.bfloat16)
+        total[...] += jnp.dot(prod, bank[group], preferred_element_type=jnp.float32)
+
+    def block(peer):
+        columns = pl.ds(pl.multiple_of(peer * shard_len, shard_len), shard_len)
+        plain, flipped = total[:lanes, columns], total[lanes:, columns]
+        return (plain + flipped * signs(plain.shape, 1)).T.astype(jnp.bfloat16)
+
+    @pl.loop(1, count)
+    def _(hop):
+        peer = lax.rem(me + hop, count)
+        back[peer] = block(peer)
+        again(hop).start()
+
+    convolved[me] = block(me)
+
+    @pl.loop(1, count)
+    def _(hop):
+        there(0, hop).wait_send()
+        there(1, hop).wait_send()
+        again(hop).wait()
+
+    @pl.when(me < count - 1)
+    def _():
+        for index in range(3):
+            rim_copy(index).wait_send()
+
+    for peer in range(count):
+        columns = slice(peer * part, (peer + 1) * part)
+        local = convolved[peer].astype(jnp.float32)[:, :part]
+        inner = local + skip_ref[:, columns] * source[:, columns]
+        gated_ref[:, columns] = (query[:, columns] * inner).astype(jnp.bfloat16)
 
 
 def on_device(
@@ -192,40 +391,55 @@
     out_weight,
 ):
     shard_len, width = query_projected.shape
-    seq_count = lax.axis_size("seq")
-    seq_len = seq_count * shard_len
-    part = width // seq_count
-    streams = [query_projected, key_stream, value_stream]
-    rims = from_behind(jnp.stack([x[-2:] for x in streams]), "seq", 1)
-
-    def shape_stream(index):
-        ext = jnp.concatenate([rims[index], streams[index]], axis=0).astype(jnp.float32)
-        return (
-            short_taps[0, index] * ext[2:]
-            + short_taps[1, index] * ext[1:-1]
-            + short_taps[2, index] * ext[:-2]
-        )
-
-    source = shape_stream(1) * shape_stream(2)
-    fields = jnp.stack([source.astype(jnp.bfloat16), long_filter.astype(jnp.bfloat16)])
-    fields = fields.reshape(2, shard_len, seq_count, part).transpose(2, 1, 0, 3)
-    fields = fields.reshape(seq_count, shard_len, 2 * part)
-    fields = lax.all_to_all(fields, "seq", 0, 0, tiled=True).reshape(seq_len, 2 * part)
-    spec = jnp.dot(matrix, fields, preferred_element_type=jnp.float32)
-    real, imag = spec[:seq_len], spec[seq_len:]
-    a, b = real[:, :part], real[:, part:]
-    c, d = imag[:, :part], imag[:, part:]
-    prod = jnp.concatenate([a * b - c * d, a * d + c * b]) * (1.0 / seq_len)
-    convolved = lax.dot_general(
+    count = lax.axis_size("seq")
+    lanes = -(-(width // count) // LANES) * LANES
+    groups, rows, seq_len = matrix.shape
+    vmem = pl.BlockSpec(memory_space=pltpu.VMEM)
+    gated = pl.pallas_call(
+        gate_kernel,
+        out_shape=jax.ShapeDtypeStruct((shard_len, width), jnp.bfloat16),
+        in_specs=[vmem] * 6 + [pl.BlockSpec(memory_space=pl.ANY)],
+        out_specs=vmem,
+        scratch_shapes=[
+            pltpu.VMEM((3, RIM, width), jnp.bfloat16),
+            pltpu.VMEM((8 + shard_len, width), jnp.float32),
+            pltpu.VMEM((shard_len, width), jnp.float32),
+            pltpu.VMEM((shard_len, width), jnp.float32),
+            pltpu.VMEM((2, count, shard_len, lanes), jnp.bfloat16),
+            pltpu.VMEM((2, count, shard_len, lanes), jnp.bfloat16),
+            pltpu.VMEM((seq_len, 2 * lanes), jnp.bfloat16),
+            pltpu.VMEM((groups, rows, seq_len), jnp.bfloat16),
+            pltpu.VMEM((groups, rows, 2 * lanes), jnp.float32),
+            pltpu.VMEM((2 * lanes, seq_len), jnp.float32),
+            pltpu.VMEM((count, shard_len, lanes), jnp.bfloat16),
+            pltpu.VMEM((count, shard_len, lanes), jnp.bfloat16),
+            pltpu.SemaphoreType.DMA((groups,)),
+            pltpu.SemaphoreType.DMA((3,)),
+            pltpu.SemaphoreType.DMA((3,)),
+            pltpu.SemaphoreType.DMA((2, count)),
+            pltpu.SemaphoreType.DMA((2, count)),
+            pltpu.SemaphoreType.DMA((count,)),
+            pltpu.SemaphoreType.DMA((count,)),
+        ],
+        compiler_params=pltpu.CompilerParams(
+            collective_id=0,
+            has_side_effects=True,
+            vmem_limit_bytes=28 * 2**20 + 2 * groups * rows * seq_len,
+        ),
+        cost_estimate=pl.CostEstimate(
+            flops=12 * groups * rows * seq_len * lanes,
+            bytes_accessed=2 * groups * rows * seq_len,
+            transcendentals=0,
+        ),
+    )(
+        query_projected,
+        key_stream,
+        value_stream,
+        short_taps,
+        skip_gain[None, :],
+        long_filter,
         matrix,
-        prod.astype(jnp.bfloat16),
-        (((0,), (0,)), ((), ())),
-        preferred_element_type=jnp.float32,
-    ).astype(jnp.bfloat16)
-    convolved = convolved.reshape(seq_count, shard_len, part)
-    convolved = lax.all_to_all(convolved, "seq", 0, 0, tiled=True)
-    convolved = convolved.transpose(1, 0, 2).reshape(shard_len, width).astype(jnp.float32)
-    gated = (shape_stream(0) * (convolved + skip_gain * source)).astype(jnp.bfloat16)
+    )
     return project(gated, out_weight)
 
 
@@ -234,7 +448,7 @@
         on_device,
         mesh=mesh,
         in_specs=(
-            P(None, None),
+            P(None, None, None),
             P("seq", "chan"),
             P("seq", "chan"),
             P("seq", "chan"),

time: 110 us -> 92.8 us (0.84)
  the two profiles are of different devices: /device:TPU:0 before, /device:TPU:29 now
where the time goes in v4:
time: 92.8 us; the launch traced here: 92.4 us
  Pallas kernels  81.8 us (88%)
  local copies, waits for them, and re-layouts  10.5 us (11%)
    pallas_call x1, Pallas kernels, on_device(): pl.pallas_call(gate_kernel, out_shape=jax.ShapeDtypeStruct((shard_len, wi...  50.4 us
    pallas_call x1, Pallas kernels, project(): pl.pallas_call(functools.partial(project_kernel, rounds), out_shape=jax.S...  31.4 us
    unnamed x17, local copies, waits for them, and re-layouts  10.5 us

profile of v4, /device:TPU:29, one launch (start us, length us, event | category | flops | bytes accessed | tf_op | source)
XLA Modules:
  0.0 92.4 jit_solution(1889381390069261998)
XLA Ops:
  0.0 0.0 copy-start.1
  0.0 1.2 %copy-done.1 = f32[256,1024]{1,0:T(8,128)S(1)} copy-done((f32[256,1024]{1,0:T(8,128)S(1)}, f32[256,1024]{1,0:T(8,128)}, u32[]{:S(2)}) %copy-start.1) | copy-done | bytes 1048600
  1.2 0.0 copy-start.2
  1.2 1.0 %copy-done.2 = bf16[256,1024]{1,0:T(8,128)(2,1)S(1)} copy-done((bf16[256,1024]{1,0:T(8,128)(2,1)S(1)}, bf16[256,1024]{1,0:T(8,128)(2,1)}, u32[]{:S(2)}) %copy-start.2) | copy-done | bytes 524312
  2.3 0.0 copy-start.3
  2.3 1.0 %copy-done.3 = bf16[256,1024]{1,0:T(8,128)(2,1)S(1)} copy-done((bf16[256,1024]{1,0:T(8,128)(2,1)S(1)}, bf16[256,1024]{1,0:T(8,128)(2,1)}, u32[]{:S(2)}) %copy-start.3) | copy-done | bytes 524312
  3.3 0.0 copy-start.4
  3.3 1.0 %copy-done.4 = bf16[256,1024]{1,0:T(8,128)(2,1)S(1)} copy-done((bf16[256,1024]{1,0:T(8,128)(2,1)S(1)}, bf16[256,1024]{1,0:T(8,128)(2,1)}, u32[]{:S(2)}) %copy-start.4) | copy-done | bytes 524312
  4.4 0.0 copy-start.5
  4.4 0.8 copy-done.5
  5.2 0.0 copy-start.6
  5.2 0.7 copy-done.6
  5.8 0.0 copy-start.7
  5.8 3.4 %copy-done.7 = bf16[4,512,2048]{2,1,0:T(8,128)(2,1)S(1)} copy-done((bf16[4,512,2048]{2,1,0:T(8,128)(2,1)S(1)}, bf16[4,512,2048]{2,1,0:T(8,128)(2,1)}, u32[]{:S(2)}) %copy-start.7) | copy-done | bytes 8388632
  9.2 0.0 copy-start
  9.2 50.4 %shard_map.82.gated_ref = bf16[256,1024]{1,0:T(8,128)(2,1)S(1)} custom-call(bf16[256,1024]{1,0:T(8,128)(2,1)S(1)} %copy-done.2, bf16[256,1024]{1,0:T(8,128)(2,1)S(1)} %copy-done.3, bf16[256,1024]{1,0:T(8,128)(2,1)S(1)} %copy-done.4, f32[3,3,1024]{2,1,0:T(4,128)S(1)} %copy-done.5, f32[1,1024]{1,0:T(1,128)S(1)} %bitcast.1, f32[256,1024]{1,0:T(8,128)S(1)} %copy-done.1, ...), custom_call_target="tpu_custom_call" | custom-call | flops 6442450944 | bytes 8388608 | tf_op jit(solution)/shard_map/pallas_call | solution.py:398
  59.6 0.0 copy-done
  59.6 31.4 %shard_map.83 = bf16[256,4096]{1,0:T(8,128)(2,1)S(1)} custom-call(bf16[256,1024]{1,0:T(8,128)(2,1)S(1)} %shard_map.82.gated_ref, bf16[1024,4096]{1,0:T(8,128)(2,1)S(1)} %copy-done), custom_call_target="tpu_custom_call" | custom-call | flops 2147483648 | bytes 12582912 | tf_op jit(solution)/shard_map/pallas_call | solution.py:154
  91.1 1.3 %copy.10 = bf16[256,4096]{1,0:T(8,128)(2,1)} copy(bf16[256,4096]{1,0:T(8,128)(2,1)S(1)} %shard_map.83) | data formatting | bytes 4194304
Async XLA Ops:
  0.0 1.2 %copy-start.1 = (f32[256,1024]{1,0:T(8,128)S(1)}, f32[256,1024]{1,0:T(8,128)}, u32[]{:S(2)}) copy-start(f32[256,1024]{1,0:T(8,128)} %filter_ref.1) | copy-start | bytes 3145732
  1.2 1.0 %copy-start.2 = (bf16[256,1024]{1,0:T(8,128)(2,1)S(1)}, bf16[256,1024]{1,0:T(8,128)(2,1)}, u32[]{:S(2)}) copy-start(bf16[256,1024]{1,0:T(8,128)(2,1)} %query_ref.1) | copy-start | bytes 1572868
  2.3 1.0 %copy-start.3 = (bf16[256,1024]{1,0:T(8,128)(2,1)S(1)}, bf16[256,1024]{1,0:T(8,128)(2,1)}, u32[]{:S(2)}) copy-start(bf16[256,1024]{1,0:T(8,128)(2,1)} %key_ref.1) | copy-start | bytes 1572868
  3.3 1.0 %copy-start.4 = (bf16[256,1024]{1,0:T(8,128)(2,1)S(1)}, bf16[256,1024]{1,0:T(8,128)(2,1)}, u32[]{:S(2)}) copy-start(bf16[256,1024]{1,0:T(8,128)(2,1)} %value_ref.1) | copy-start | bytes 1572868
  4.4 0.8 copy-start.5
  5.2 0.7 copy-start.6
  5.8 3.4 %copy-start.7 = (bf16[4,512,2048]{2,1,0:T(8,128)(2,1)S(1)}, bf16[4,512,2048]{2,1,0:T(8,128)(2,1)}, u32[]{:S(2)}) copy-start(bf16[4,512,2048]{2,1,0:T(8,128)(2,1)} %constant.2.clone.matrix_ref) | copy-start | bytes 25165828
  9.2 50.4 %copy-start = (bf16[1024,4096]{1,0:T(8,128)(2,1)S(1)}, bf16[1024,4096]{1,0:T(8,128)(2,1)}, u32[]{:S(2)}) copy-start(bf16[1024,4096]{1,0:T(8,128)(2,1)} %weight_ref.1) | copy-start | bytes 25165828

commit v5 on v4

--- a/solution.py
+++ b/solution.py
@@ -171,7 +171,7 @@
             pltpu.SemaphoreType.DMA((CHUNKS,)),
         ],
         compiler_params=pltpu.CompilerParams(
-            collective_id=1, has_side_effects=True, vmem_limit_bytes=32 * 2**20
+            collective_id=1, has_side_effects=True, vmem_limit_bytes=60 * 2**20
         ),
         cost_estimate=pl.CostEstimate(
             flops=2 * rows * depth * columns,
@@ -185,11 +185,14 @@
     query_ref,
     key_ref,
     value_ref,
-    taps_ref,
-    skip_ref,
+    taps_in_ref,
+    skip_in_ref,
     filter_ref,
     matrix_ref,
     gated_ref,
+    held,
+    taps_ref,
+    skip_ref,
     rim,
     extended,
     query,
@@ -202,6 +205,7 @@
     total,
     back,
     convolved,
+    held_sem,
     bank_sem,
     rim_send_sem,
     rim_recv_sem,
@@ -216,6 +220,22 @@
     me = lax.axis_index("seq")
     streams = (query_ref, key_ref, value_ref)
 
+    loads = [
+        pltpu.make_async_copy(src, dst, held_sem.at[place])
+        for place, (src, dst) in enumerate(
+            [
+                (filter_ref, source),
+                (taps_in_ref, taps_ref),
+                (key_ref, held.at[1]),
+                (value_ref, held.at[2]),
+                (query_ref, held.at[0]),
+                (skip_in_ref, skip_ref),
+            ]
+        )
+    ]
+    for load in loads:
+        load.start()
+
     def bank_copy(group):
         return pltpu.make_async_copy(matrix_ref.at[group], bank.at[group], bank_sem.at[group])
 
@@ -285,7 +305,7 @@
 
     def shaped(index):
         extended[:8] = rim[index].astype(jnp.float32)[RIM - 8 :]
-        extended[8:] = streams[index][...].astype(jnp.float32)
+        extended[8:] = held[index].astype(jnp.float32)
         result = taps_ref[0, index : index + 1] * extended[8:]
         for tap in (1, 2):
             rows = extended[8 - tap : 8 - tap + shard_len]
@@ -299,7 +319,8 @@
         peer = lax.rem(me + hop, count)
         pl.semaphore_signal(barrier, inc=1, device_id={"seq": peer}, device_id_type=MESH)
 
-    split(0, filter_ref)
+    loads[0].wait()
+    split(0, source)
     pl.semaphore_wait(barrier, count - 1)
 
     @pl.when(me < count - 1)
@@ -322,6 +343,8 @@
         for index in range(3):
             rim_copy(index).wait_recv()
 
+    for load in loads[1:]:
+        load.wait()
     source[...] = shaped(1)
     source[...] = source[...] * shaped(2)
     split(1, source)
@@ -398,9 +421,12 @@
     gated = pl.pallas_call(
         gate_kernel,
         out_shape=jax.ShapeDtypeStruct((shard_len, width), jnp.bfloat16),
-        in_specs=[vmem] * 6 + [pl.BlockSpec(memory_space=pl.ANY)],
+        in_specs=[pl.BlockSpec(memory_space=pl.ANY)] * 7,
         out_specs=vmem,
         scratch_shapes=[
+            pltpu.VMEM((3, shard_len, width), jnp.bfloat16),
+            pltpu.VMEM(short_taps.shape, jnp.float32),
+            pltpu.VMEM((1, width), jnp.float32),
             pltpu.VMEM((3, RIM, width), jnp.bfloat16),
             pltpu.VMEM((8 + shard_len, width), jnp.float32),
             pltpu.VMEM((shard_len, width), jnp.float32),
@@ -413,6 +439,7 @@
             pltpu.VMEM((2 * lanes, seq_len), jnp.float32),
             pltpu.VMEM((count, shard_len, lanes), jnp.bfloat16),
             pltpu.VMEM((count, shard_len, lanes), jnp.bfloat16),
+            pltpu.SemaphoreType.DMA((6,)),
             pltpu.SemaphoreType.DMA((groups,)),
             pltpu.SemaphoreType.DMA((3,)),
             pltpu.SemaphoreType.DMA((3,)),
@@ -424,7 +451,7 @@
         compiler_params=pltpu.CompilerParams(
             collective_id=0,
             has_side_effects=True,
-            vmem_limit_bytes=28 * 2**20 + 2 * groups * rows * seq_len,
+            vmem_limit_bytes=60 * 2**20,
         ),
         cost_estimate=pl.CostEstimate(
             flops=12 * groups * rows * seq_len * lanes,

time: 92.8 us -> 88 us (0.948)
  local copies, waits for them, and re-layouts: 10.5 us -> 3.13 us
  Pallas kernels: 81.8 us -> 84.7 us
    unnamed x17 -> x1, local copies, waits for them, and re-layouts: 10.5 us -> 3.13 us
    pallas_call x1, Pallas kernels: 31.4 us -> 33.3 us  [project(): pl.pallas_call(functools.partial(project_kernel, rounds), out_shape=jax.S...]
    pallas_call x1, Pallas kernels: 50.4 us -> 51.4 us  [on_device(): pl.pallas_call(gate_kernel, out_shape=jax.ShapeDtypeStruct((shard_len, wi...]
where the time goes in v5:
time: 88 us; the launch traced here: 87.8 us
  Pallas kernels  84.7 us (96%)
  local copies, waits for them, and re-layouts  3.13 us (4%)
    pallas_call x1, Pallas kernels, on_device(): pl.pallas_call(gate_kernel, out_shape=jax.ShapeDtypeStruct((shard_len, wi...  51.4 us
    pallas_call x1, Pallas kernels, project(): pl.pallas_call(functools.partial(project_kernel, rounds), out_shape=jax.S...  33.3 us
    unnamed x1, local copies, waits for them, and re-layouts  3.13 us

profile of v5, /device:TPU:29, one launch (start us, length us, event | category | flops | bytes accessed | tf_op | source)
XLA Modules:
  0.0 87.8 jit_solution(2019431052397332740)
XLA Ops:
  0.0 51.4 %shard_map.82.gated_ref = bf16[256,1024]{1,0:T(8,128)(2,1)} custom-call(bf16[256,1024]{1,0:T(8,128)(2,1)} %query_ref.1, bf16[256,1024]{1,0:T(8,128)(2,1)} %key_ref.1, bf16[256,1024]{1,0:T(8,128)(2,1)} %value_ref.1, f32[3,3,1024]{2,1,0:T(4,128)} %taps_in_ref.1, f32[1,1024]{1,0:T(1,128)} %bitcast.1, f32[256,1024]{1,0:T(8,128)} %filter_ref.1, ...), custom_call_target="tpu_custom_call" | custom-call | flops 6442450944 | bytes 8388608 | tf_op jit(solution)/shard_map/pallas_call | solution.py:421
  51.4 33.3 %shard_map.83 = bf16[256,4096]{1,0:T(8,128)(2,1)} custom-call(bf16[256,1024]{1,0:T(8,128)(2,1)} %shard_map.82.gated_ref, bf16[1024,4096]{1,0:T(8,128)(2,1)} %weight_ref.1), custom_call_target="tpu_custom_call" | custom-call | flops 2147483648 | bytes 12582912 | tf_op jit(solution)/shard_map/pallas_call | solution.py:154
  84.7 3.1 %copy.10 = bf16[256,4096]{1,0:T(8,128)(2,1)} copy(bf16[256,4096]{1,0:T(8,128)(2,1)} %shard_map.83) | data formatting | bytes 4194304

commit v6 on v5

--- a/solution.py
+++ b/solution.py
@@ -25,7 +25,7 @@
     return groups.transpose(1, 0, 2, 3).reshape(-1, 2 * FREQS, seq_len)
 
 
-CHUNKS = 4
+CHUNKS = 8
 MESH = pl.DeviceIdType.MESH
 
 
@@ -96,8 +96,8 @@
             device_id_type=MESH,
         )
 
-    for turn in range(2):
-        for j in range(CHUNKS):
+    for j in range(CHUNKS):
+        for turn in range(2):
             weight_copy(turn, j).start()
     barrier = pltpu.get_barrier_semaphore()
     for peer in [mate] + [chip_peer(step) for step in range(rounds)]:
@@ -111,13 +111,18 @@
             gated_ref[...], weight[:, cols(side, j)], preferred_element_type=jnp.float32
         )
 
+    def give(j):
+        core_send[j] = part(0, j)
+        core_copy(j).start()
+
+    give(0)
+
     @pl.loop(0, CHUNKS)
     def _(j):
-        core_send[j] = part(0, j)
-        core_copy(j).start()
-
-    @pl.loop(0, CHUNKS)
-    def _(j):
+        @pl.when(j + 1 < CHUNKS)
+        def _():
+            give(j + 1)
+
         own = part(1, j)
         core_copy(j).wait_recv()
         chip_send[0, j] = (own + core_recv[j]).astype(jnp.bfloat16)

time: 88 us -> 87.2 us (level)
  Pallas kernels: 84.7 us -> 83.8 us
where the time goes in v6:
time: 87.2 us; the launch traced here: 87 us
  Pallas kernels  83.8 us (96%)
  local copies, waits for them, and re-layouts  3.13 us (4%)
    pallas_call x1, Pallas kernels, on_device(): pl.pallas_call(gate_kernel, out_shape=jax.ShapeDtypeStruct((shard_len, wi...  51.4 us
    pallas_call x1, Pallas kernels, project(): pl.pallas_call(functools.partial(project_kernel, rounds), out_shape=jax.S...  32.5 us
    unnamed x1, local copies, waits for them, and re-layouts  3.13 us

profile of v6, /device:TPU:29, one launch (start us, length us, event | category | flops | bytes accessed | tf_op | source)
XLA Modules:
  0.0 87.0 jit_solution(4746488947350192799)
XLA Ops:
  0.0 51.4 %shard_map.82.gated_ref = bf16[256,1024]{1,0:T(8,128)(2,1)} custom-call(bf16[256,1024]{1,0:T(8,128)(2,1)} %query_ref.1, bf16[256,1024]{1,0:T(8,128)(2,1)} %key_ref.1, bf16[256,1024]{1,0:T(8,128)(2,1)} %value_ref.1, f32[3,3,1024]{2,1,0:T(4,128)} %taps_in_ref.1, f32[1,1024]{1,0:T(1,128)} %bitcast.1, f32[256,1024]{1,0:T(8,128)} %filter_ref.1, ...), custom_call_target="tpu_custom_call" | custom-call | flops 6442450944 | bytes 8388608 | tf_op jit(solution)/shard_map/pallas_call | solution.py:426
  51.4 32.5 %shard_map.83 = bf16[256,4096]{1,0:T(8,128)(2,1)} custom-call(bf16[256,1024]{1,0:T(8,128)(2,1)} %shard_map.82.gated_ref, bf16[1024,4096]{1,0:T(8,128)(2,1)} %weight_ref.1), custom_call_target="tpu_custom_call" | custom-call | flops 2147483648 | bytes 12582912 | tf_op jit(solution)/shard_map/pallas_call | solution.py:159
  83.8 3.1 %copy.10 = bf16[256,4096]{1,0:T(8,128)(2,1)} copy(bf16[256,4096]{1,0:T(8,128)(2,1)} %shard_map.83) | data formatting | bytes 4194304
